TPU v7x, 128 devices: a whole 4x4x4 slice. The times are simulated.
128 devices in a mesh: row: 16 (over z, x), col: 8 (over y, core).
Axes of the slice: x: 4, y: 4, z: 4, core: 2. Of those that a mesh axis runs over, the one named last changes fastest.
Arguments:
- matrix_blocks: float32 [8, 16, 16, 8, 128, 128], P(None, 'row', None, 'col'), as said below
- pattern: int32 [128, 128], replicated, may hold values from 0 to 1, as said below
- order: int32 [128], replicated, may hold values from 0 to 127, each once
Outputs:
- panels: bfloat16 [2, 8, 16, 128, 512], P(None, None, 'row')
- trailing: float32 [8, 16, 16, 8, 128, 128], P(None, 'row', None, 'col')
Inputs may be any that keep to these rules, and one draw needn't show every extreme that they name: The blocks fall into 8 nonempty clusters, and pattern[g, h] is 1 exactly where blocks g and h lie in the same cluster. `matrix_blocks`: symmetric as a 16384 x 16384 matrix and positive definite, also after masking by any such pattern.
All inputs are finite; a program needn't handle non-finite values.
Results may differ from a plain program's by a relative error of at most 0.0022.
Values may be sent and summed in bfloat16 or wider, within the bound.
A program may use at most 128 MiB of HBM per device.

v0:
```python
import jax
import jax.numpy as jnp
from jax import lax
from jax.sharding import PartitionSpec as P

SUPER = 4


def broadcast(value, axis, source):
    kept = jnp.where(lax.axis_index(axis) == source, value, 0).astype(value.dtype)
    return lax.psum(kept, axis)


def shards(matrix_blocks, pattern, order):
    rows_axis = lax.axis_size("row")
    cols_axis = lax.axis_size("col")
    my_row = lax.axis_index("row")
    my_col = lax.axis_index("col")
    row_blocks = matrix_blocks.shape[0]
    col_blocks = matrix_blocks.shape[2]
    width = matrix_blocks.shape[4]
    ratio = rows_axis // cols_axis
    total_blocks = row_blocks * rows_axis
    local = matrix_blocks[:, 0, :, 0]
    my_pattern = lax.dynamic_index_in_dim(
        pattern.reshape(row_blocks, rows_axis, total_blocks), my_row, 1, keepdims=False
    )
    my_pattern = lax.dynamic_index_in_dim(
        my_pattern.reshape(row_blocks, col_blocks, cols_axis), my_col, 2, keepdims=False
    )
    current = local * my_pattern.astype(jnp.float32)[:, :, None, None]
    dead = jnp.zeros((total_blocks,), jnp.float32)
    results = []
    for step in range(2):
        chosen = order[step * SUPER : (step + 1) * SUPER]
        pieces = []
        for member in range(SUPER):
            target = chosen[member]
            column_here = lax.dynamic_index_in_dim(current, target // cols_axis, 1, keepdims=False)
            pieces.append(broadcast(column_here, "col", target % cols_axis))
        panel = jnp.concatenate(pieces, axis=2)
        parts_list = []
        for member in range(SUPER):
            target = chosen[member]
            row_here = lax.dynamic_index_in_dim(panel, target // rows_axis, 0, keepdims=False)
            parts_list.append(
                jnp.where(target % rows_axis == my_row, row_here, jnp.zeros_like(row_here))
            )
        square = lax.psum(jnp.concatenate(parts_list, axis=0), "row")
        factor = jnp.linalg.cholesky(square)
        flat = panel.reshape(row_blocks * width, SUPER * width)
        lower = lax.linalg.triangular_solve(
            factor, flat, left_side=False, lower=True, transpose_a=True
        )
        dead = dead.at[chosen].set(1.0)
        alive = lax.dynamic_index_in_dim(
            (1.0 - dead).reshape(row_blocks, rows_axis), my_row, 1, keepdims=False
        )
        rounded = (lower.reshape(row_blocks, width, SUPER * width) * alive[:, None, None]).astype(
            jnp.bfloat16
        )
        results.append(rounded)
        whole = lax.all_gather(rounded, "row", axis=0, tiled=True)
        whole = whole.reshape(ratio, cols_axis, row_blocks, width, SUPER * width)
        picked = lax.dynamic_index_in_dim(whole, my_col, 1, keepdims=False)
        column_panel = picked.transpose(1, 0, 2, 3).reshape(col_blocks, width, SUPER * width)
        update = jnp.einsum(
            "aik,cjk->acij", rounded, column_panel, preferred_element_type=jnp.float32
        )
        current = current - update
    panels = jnp.stack(results)[:, :, None]
    return (panels, current[:, None, :, None])


def solution(mesh):
    in_specs = (P(None, "row", None, "col", None, None), P(), P())
    out_specs = (P(None, None, "row", None, None), P(None, "row", None, "col", None, None))
    return jax.shard_map(shards, mesh=mesh, in_specs=in_specs, out_specs=out_specs, check_vma=False)
```

profile of v0, /device:TPU:3, one launch (start us, length us, event | category | flops | bytes accessed | tf_op | source)
XLA Modules:
  0.0 961.4 jit_solution(18125516481466033667)
XLA Ops:
  39.1 66.3 %all-reduce.14.cloned.1.call-done = (f32[8,128,128]{1,2,0:T(8,128)}, f32[8,128,128]{1,2,0:T(8,128)}, f32[8,128,128]{1,2,0:T(8,128)}, f32[8,128,128]{1,2,0:T(8,128)}) async-done(((f32[8,128,128]{1,2,0:T(8,128)}, f32[8,128,128]{1,2,0:T(8,128)}, f32[8,128,128]{1,2,0:T(8,128)}, f32[8,128,128]{1,2,0:T(8,128)}), (f32[8,128,128]{1,2,0:T(8,128)}, f32[8,128,128]{1,2,0:T(8,128)}, f32[8,128,128]{1,2,0:T(8,128)}, ...) | async-done | bytes 2097168 | tf_op jit(solution)/shard_map/psum | solution.py:11
  113.6 83.7 %all-reduce.8.cloned.1.call-done = f32[512,512]{0,1:T(8,128)} async-done(((f32[512,512]{0,1:T(8,128)}), f32[512,512]{0,1:T(8,128)}) %all-reduce.8.cloned.1.call-update) | async-done | bytes 1048592 | tf_op jit(solution)/shard_map/psum | solution.py:49
  202.3 11.7 %cholesky.286 = f32[128,128]{1,0:T(8,128)S(1)} custom-call(f32[128,128]{1,0:T(8,128)S(1)} %cholesky.426), custom_call_target="Cholesky" | custom-call | tf_op jit(solution)/shard_map/jit(cholesky)/cholesky | solution.py:50
  214.2 9.8 %custom-call.27 = f32[1,128,128]{1,2,0:T(8,128)S(1)} custom-call(f32[1,128,128]{2,1,0:T(8,128)S(1)} %get-tuple-element.95), custom_call_target="InvertDiagBlocksLowerTriangular" | custom-call | tf_op jit(solution)/shard_map/jit(cholesky)/cholesky | solution.py:50
  226.5 11.7 %cholesky.305 = f32[128,128]{1,0:T(8,128)S(1)} custom-call(f32[128,128]{1,0:T(8,128)S(1)} %cholesky.430), custom_call_target="Cholesky" | custom-call | tf_op jit(solution)/shard_map/jit(cholesky)/cholesky | solution.py:50
  238.3 10.2 %custom-call.28 = f32[1,128,128]{1,2,0:T(8,128)S(1)} custom-call(f32[1,128,128]{2,1,0:T(8,128)S(1)} %get-tuple-element.92), custom_call_target="InvertDiagBlocksLowerTriangular" | custom-call | tf_op jit(solution)/shard_map/jit(cholesky)/cholesky | solution.py:50
  250.0 11.7 %cholesky.326 = f32[128,128]{1,0:T(8,128)S(1)} custom-call(f32[128,128]{1,0:T(8,128)S(1)} %cholesky.435), custom_call_target="Cholesky" | custom-call | tf_op jit(solution)/shard_map/jit(cholesky)/cholesky | solution.py:50
  261.8 9.8 %custom-call.29 = f32[1,128,128]{1,2,0:T(8,128)S(1)} custom-call(f32[1,128,128]{2,1,0:T(8,128)S(1)} %get-tuple-element.89), custom_call_target="InvertDiagBlocksLowerTriangular" | custom-call | tf_op jit(solution)/shard_map/jit(cholesky)/cholesky | solution.py:50
  273.0 11.7 %cholesky.343 = f32[128,128]{1,0:T(8,128)S(1)} custom-call(f32[128,128]{1,0:T(8,128)S(1)} %convolution_subtract_fusion.9), custom_call_target="Cholesky" | custom-call | tf_op jit(solution)/shard_map/jit(cholesky)/cholesky | solution.py:50
  290.6 11.9 %while.4 = (s32[]{:T(128)}, f32[512,512]{1,0:T(8,128)}, s32[4,2]{0,1:T(2,128)S(1)}, f32[4,128,128]{2,1,0:T(8,128)S(1)}, s32[]{:T(128)}) while((s32[]{:T(128)}, f32[512,512]{1,0:T(8,128)}, s32[4,2]{0,1:T(2,128)S(1)}, f32[4,128,128]{2,1,0:T(8,128)S(1)}, s32[]{:T(128)}) %tuple.83), condition=%wide.while_cond, body=%wide.while_body.sunk | while | flops 2 | bytes 131189 | solution.py:52
  302.4 39.3 %custom-call.30 = f32[4,128,128]{1,2,0:T(8,128)S(1)} custom-call(f32[4,128,128]{2,1,0:T(8,128)S(1)} %get-tuple-element.18), custom_call_target="InvertDiagBlocksLowerTriangular" | custom-call | tf_op jit(solution)/shard_map/triangular_solve/custom-call.3 | solution.py:52
  366.2 109.7 %all-gather.3.cloned.1.call-done = bf16[128,128,512]{1,0,2:T(8,128)(2,1)} async-done(((bf16[8,128,512]{1,0,2:T(8,128)(2,1)}), bf16[128,128,512]{1,0,2:T(8,128)(2,1)}) %all-gather.3.cloned.1.call-update) | async-done | bytes 16777232 | tf_op jit(solution)/shard_map/all_gather | solution.py:63
  494.4 64.5 %all-reduce.12.cloned.1.call-done = (f32[8,128,128]{1,2,0:T(8,128)}, f32[8,128,128]{1,2,0:T(8,128)}, f32[8,128,128]{1,2,0:T(8,128)}, f32[8,128,128]{1,2,0:T(8,128)}) async-done(((f32[8,128,128]{1,2,0:T(8,128)}, f32[8,128,128]{1,2,0:T(8,128)}, f32[8,128,128]{1,2,0:T(8,128)}, f32[8,128,128]{1,2,0:T(8,128)}), (f32[8,128,128]{1,2,0:T(8,128)}, f32[8,128,128]{1,2,0:T(8,128)}, f32[8,128,128]{1,2,0:T(8,128)}, ...) | async-done | bytes 2097168 | tf_op jit(solution)/shard_map/psum | solution.py:11
  568.0 82.5 %all-reduce.10.cloned.1.call-done = f32[512,512]{0,1:T(8,128)} async-done(((f32[512,512]{0,1:T(8,128)}), f32[512,512]{0,1:T(8,128)}) %all-reduce.10.cloned.1.call-update) | async-done | bytes 1048592 | tf_op jit(solution)/shard_map/psum | solution.py:49
  655.6 11.7 %cholesky.358 = f32[128,128]{1,0:T(8,128)S(1)} custom-call(f32[128,128]{1,0:T(8,128)S(1)} %cholesky.439), custom_call_target="Cholesky" | custom-call | tf_op jit(solution)/shard_map/jit(cholesky)/cholesky | solution.py:50
  667.5 9.8 %custom-call.31 = f32[1,128,128]{1,2,0:T(8,128)S(1)} custom-call(f32[1,128,128]{2,1,0:T(8,128)S(1)} %get-tuple-element.85), custom_call_target="InvertDiagBlocksLowerTriangular" | custom-call | tf_op jit(solution)/shard_map/jit(cholesky)/cholesky | solution.py:50
  679.8 11.7 %cholesky.377 = f32[128,128]{1,0:T(8,128)S(1)} custom-call(f32[128,128]{1,0:T(8,128)S(1)} %cholesky.443), custom_call_target="Cholesky" | custom-call | tf_op jit(solution)/shard_map/jit(cholesky)/cholesky | solution.py:50
  691.6 10.0 %custom-call.32 = f32[1,128,128]{1,2,0:T(8,128)S(1)} custom-call(f32[1,128,128]{2,1,0:T(8,128)S(1)} %get-tuple-element.82), custom_call_target="InvertDiagBlocksLowerTriangular" | custom-call | tf_op jit(solution)/shard_map/jit(cholesky)/cholesky | solution.py:50
  703.1 11.7 %cholesky.398 = f32[128,128]{1,0:T(8,128)S(1)} custom-call(f32[128,128]{1,0:T(8,128)S(1)} %cholesky.448), custom_call_target="Cholesky" | custom-call | tf_op jit(solution)/shard_map/jit(cholesky)/cholesky | solution.py:50
  714.8 9.8 %custom-call.33 = f32[1,128,128]{1,2,0:T(8,128)S(1)} custom-call(f32[1,128,128]{2,1,0:T(8,128)S(1)} %get-tuple-element.79), custom_call_target="InvertDiagBlocksLowerTriangular" | custom-call | tf_op jit(solution)/shard_map/jit(cholesky)/cholesky | solution.py:50
  726.1 11.7 %cholesky.415 = f32[128,128]{1,0:T(8,128)S(1)} custom-call(f32[128,128]{1,0:T(8,128)S(1)} %convolution_subtract_fusion.8), custom_call_target="Cholesky" | custom-call | tf_op jit(solution)/shard_map/jit(cholesky)/cholesky | solution.py:50
  744.2 11.4 %while.5 = (s32[]{:T(128)}, f32[512,512]{1,0:T(8,128)}, s32[4,2]{0,1:T(2,128)S(1)}, f32[4,128,128]{2,1,0:T(8,128)S(1)}, s32[]{:T(128)}) while((s32[]{:T(128)}, f32[512,512]{1,0:T(8,128)}, s32[4,2]{0,1:T(2,128)S(1)}, f32[4,128,128]{2,1,0:T(8,128)S(1)}, s32[]{:T(128)}) %tuple.103), condition=%wide.while_cond.clone, body=%wide.while_body.clone.sunk | while | flops 2 | bytes 131189 | solution.py:52
  755.6 39.3 %custom-call.34 = f32[4,128,128]{1,2,0:T(8,128)S(1)} custom-call(f32[4,128,128]{2,1,0:T(8,128)S(1)} %get-tuple-element.19), custom_call_target="InvertDiagBlocksLowerTriangular" | custom-call | tf_op jit(solution)/shard_map/triangular_solve/custom-call.3 | solution.py:52
  821.9 110.0 %all-gather.5.cloned.1.call-done = bf16[128,128,512]{1,0,2:T(8,128)(2,1)} async-done(((bf16[8,128,512]{1,0,2:T(8,128)(2,1)}), bf16[128,128,512]{1,0,2:T(8,128)(2,1)}) %all-gather.5.cloned.1.call-update) | async-done | bytes 16777232 | tf_op jit(solution)/shard_map/all_gather | solution.py:63
  (189 shorter events, 172.2 us)
Async XLA Ops:
  7.2 21.1 %copy-start = (s32[128,128]{1,0:T(8,128)S(1)}, s32[128,128]{1,0:T(8,128)}, u32[]{:S(2)}) copy-start(s32[128,128]{1,0:T(8,128)} %param.7) | copy-start | bytes 196612
  7.2 98.3 %all-reduce.14.cloned.1.call-start = ((), (), s32[]{:S(2)}) async-start(), calls=%async_computation.5 | async-start | bytes 4194304 | tf_op jit(solution)/shard_map/psum | solution.py:11
  39.0 158.3 %all-reduce.8.cloned.1.call-start = ((), (), s32[]{:S(2)}) async-start(), calls=%async_computation | async-start | bytes 2097152 | tf_op jit(solution)/shard_map/psum | solution.py:49
  105.5 2.3 copy-start.18
  105.5 2.3 copy-start.17
  107.8 1.3 copy-start.6
  109.2 1.2 copy-start.19
  110.4 365.6 %all-gather.3.cloned.1.call-start = ((), (), s32[]{:S(2)}) async-start(), calls=%async_computation.1 | async-start | bytes 17825792 | tf_op jit(solution)/shard_map/all_gather | solution.py:63
  197.2 2.6 copy-start.8
  354.8 204.1 %all-reduce.12.cloned.1.call-start = ((), (), s32[]{:S(2)}) async-start(), calls=%async_computation.4 | async-start | bytes 4194304 | tf_op jit(solution)/shard_map/psum | solution.py:11
  479.2 4.4 copy-start.11
  489.4 3.4 copy-start.2
  494.2 156.4 %all-reduce.10.cloned.1.call-start = ((), (), s32[]{:S(2)}) async-start(), calls=%async_computation.2 | async-start | bytes 2097152 | tf_op jit(solution)/shard_map/psum | solution.py:49
  558.8 2.3 copy-start.16
  558.8 2.3 copy-start.15
  561.2 1.3 copy-start.7
  563.7 368.3 %all-gather.5.cloned.1.call-start = ((), (), s32[]{:S(2)}) async-start(), calls=%async_computation.3 | async-start | bytes 17825792 | tf_op jit(solution)/shard_map/all_gather | solution.py:63
  650.5 2.6 copy-start.9
  795.0 4.6 copy-start.4
  812.6 3.0 copy-start.3
  817.7 2.0 copy-start.5
  819.1 1.4 copy-start.12
  935.3 3.1 copy-start.10
  945.1 9.2 copy-start.1
  (2 other events, 1.9 us)
Sparse Core Ops, SparseCore 0:
  39.1 66.3 all-reduce.13
  110.5 86.6 all-reduce.7
  354.9 121.0 all-gather.2
  494.3 64.5 all-reduce.11
  563.8 86.6 all-reduce.9
  810.9 121.0 all-gather.4
where the time goes:
time: 967 us; the launch traced here: 961 us
  waiting for transfers between devices  517 us (53%)
  other arithmetic  266 us (28%)
  local copies, waits for them, and re-layouts  91.5 us (9%)
  matrix products  46.4 us (5%)
  between operations  40.6 us (4%)
    all_gather x2, waiting for transfers between devices, shards(): whole = lax.all_gather(rounded, 'row', axis=0, tiled=True)  220 us
    psum x2, waiting for transfers between devices, shards(): square = lax.psum(jnp.concatenate(parts_list, axis=0), 'row')  166 us
    another operation x29, other arithmetic, shards(): factor = jnp.linalg.cholesky(square)  158 us
    psum x2, waiting for transfers between devices, broadcast(): return lax.psum(kept, axis)  131 us
    another operation x5, other arithmetic, shards(): lax.linalg.triangular_solve(factor, flat, left_side=False, lower=True, tr...  81.7 us
    unnamed x50, local copies, waits for them, and re-layouts  33 us
    another operation x27, local copies, waits for them, and re-layouts, shards(): lax.linalg.triangular_solve(factor, flat, left_side=False, lower=True, tr...  23.1 us
    another operation x14, matrix products, shards(): lax.linalg.triangular_solve(factor, flat, left_side=False, lower=True, tr...  23 us
  transfers between devices with their start and end apart: 6, of which 6 were waited for; matrix products, arithmetic and copies ran while one was open for 2% of the time, Pallas kernels for 0%

commit v1 on v0

v1 whole, which is shorter than its diff:
```python
import functools

import jax
import jax.numpy as jnp
from jax import lax
from jax.experimental import pallas as pl
from jax.experimental.pallas import tpu as pltpu
from jax.sharding import PartitionSpec as P

SUPER = 4
PICKS = 8
KR = 24
KD = 24
MESH = pl.DeviceIdType.MESH
HIGH = lax.Precision.HIGHEST
F32 = jnp.float32
BF16 = jnp.bfloat16
NT = (((1,), (1,)), ((), ()))

POS = 0
POSC = 64
ALIVE = 192
SAME = 256
POSD = 320
TARGET = 384
LEVEL = 392
FIRST = 400
DEPTH = 408
HIT = 416


def dot_nt(a, b):
    return lax.dot_general(a, b, NT, precision=HIGH, preferred_element_type=F32)


def pick_kernel(meta, a_ref, out_ref, sems):
    my_col = lax.axis_index("col")
    out_ref[...] = jnp.zeros_like(out_ref)

    def copy(p):
        slot = jnp.maximum(meta[POS + p], 0)
        target = meta[TARGET + p % PICKS]
        mine = (meta[POS + p] >= 0) & (target % 8 == my_col)
        return mine, pltpu.make_async_copy(
            a_ref.at[p // PICKS, target // 8], out_ref.at[:, slot], sems.at[slot]
        )

    @pl.loop(0, 64)
    def _(p):
        mine, c = copy(p)

        @pl.when(mine)
        def _():
            c.start()

    @pl.loop(0, 64)
    def _(p):
        mine, c = copy(p)

        @pl.when(mine)
        def _():
            c.wait()


def pick(meta, blocks):
    return pl.pallas_call(
        pick_kernel,
        out_shape=jax.ShapeDtypeStruct((8, KR, 16, 128), F32),
        in_specs=[pl.BlockSpec(memory_space=pltpu.SMEM), pl.BlockSpec(memory_space=pl.ANY)],
        out_specs=pl.BlockSpec(memory_space=pltpu.VMEM),
        scratch_shapes=[pltpu.SemaphoreType.DMA((KR,))],
        compiler_params=pltpu.CompilerParams(vmem_limit_bytes=16 << 20),
        name="pick",
    )(meta, blocks)


def place():
    r = lax.axis_index("row")
    c = lax.axis_index("col")
    return r, c, c // 2, c % 2


def gather_kernel(
    dl_ref, give_ref, x_ref, d_ref, ra, acc, rb, dsrc, rr, piece,
    sa, qa, sb, qb, sc, qc, sd, qd, se, qe, sf, qf,
):
    r, c, y, k = place()
    other = {"row": r, "col": y * 2 + 1 - k}

    def along(dy):
        return {"row": r, "col": lax.rem(y + dy, 4) * 2 + k}

    def across(dr):
        return {"row": lax.rem(r + dr, 16), "col": c}

    barrier = pltpu.get_barrier_semaphore()
    pl.semaphore_signal(barrier, inc=1, device_id=other, device_id_type=MESH)
    for dy in (1, 2, 3):
        pl.semaphore_signal(barrier, inc=1, device_id=along(dy), device_id_type=MESH)
    for dr in range(1, 16):
        pl.semaphore_signal(barrier, inc=1, device_id=across(dr), device_id_type=MESH)
    pl.semaphore_wait(barrier, 19)

    halves = []
    for dy in (2, 1, 3, 0):
        there = lax.rem(y + dy, 4)
        h = pltpu.make_async_remote_copy(
            src_ref=give_ref.at[there, 1 - k], dst_ref=ra.at[dy],
            send_sem=sa.at[dy], recv_sem=qa.at[dy], device_id=other, device_id_type=MESH,
        )
        h.start()
        halves.append((dy, there, h))
    quarters = []
    for dy, there, h in halves:
        h.wait_recv()
        if dy:
            acc[dy] = give_ref[there, k] + ra[dy]
            q = pltpu.make_async_remote_copy(
                src_ref=acc.at[dy], dst_ref=rb.at[dy],
                send_sem=sb.at[dy], recv_sem=qb.at[dy], device_id=along(dy), device_id_type=MESH,
            )
            q.start()
            quarters.append((dy, q))
        else:
            total = give_ref[there, k] + ra[dy]
    for dy, q in quarters:
        q.wait_recv()
        total = total + rb[dy]
    x_ref[...] = total

    for d in range(KD):
        code = dl_ref[d]
        mine = (code // 64 == r).astype(F32)
        dsrc[d * 16 : (d + 1) * 16] = x_ref[code % 64] * mine
    parts = []
    for dr in range(1, 16):
        there = lax.rem(r + dr, 16)
        h = pltpu.make_async_remote_copy(
            src_ref=dsrc.at[pl.ds(there * KD, KD)], dst_ref=rr.at[dr],
            send_sem=sc.at[dr], recv_sem=qc.at[dr], device_id=across(dr), device_id_type=MESH,
        )
        h.start()
        parts.append(h)
    total = dsrc[pl.ds(pl.multiple_of(r * KD, 8), KD)]
    for dr, h in zip(range(1, 16), parts):
        h.wait_recv()
        total = total + rr[dr]
    piece[...] = total
    mine = pl.ds(pl.multiple_of(r * KD, 8), KD)
    d_ref[y, k, mine] = total
    wholes = []
    for dr in range(1, 16):
        h = pltpu.make_async_remote_copy(
            src_ref=piece, dst_ref=d_ref.at[y, k, mine],
            send_sem=sd.at[dr], recv_sem=qd.at[dr], device_id=across(dr), device_id_type=MESH,
        )
        h.start()
        wholes.append(h)
    for h in wholes:
        h.wait_recv()
    spread(d_ref, along, other, y, k, se, qe, sf, qf)
    for _, _, h in halves:
        h.wait_send()
    for _, q in quarters:
        q.wait_send()
    for h in parts + wholes:
        h.wait_send()


def spread(ref, along, other, y, k, se, qe, sf, qf):
    outs = []
    for dy in (2, 1, 3):
        h = pltpu.make_async_remote_copy(
            src_ref=ref.at[y, k], dst_ref=ref.at[y, k],
            send_sem=se.at[dy], recv_sem=qe.at[dy], device_id=along(dy), device_id_type=MESH,
        )
        h.start()
        outs.append((dy, h))
    twins = []
    for dy in (0, 1, 3, 2):
        come = lax.rem(y + 4 - dy, 4)
        for d, h in outs:
            if d == dy:
                h.wait_recv()
        t = pltpu.make_async_remote_copy(
            src_ref=ref.at[come, k], dst_ref=ref.at[come, k],
            send_sem=sf.at[dy], recv_sem=qf.at[dy], device_id=other, device_id_type=MESH,
        )
        t.start()
        twins.append(t)
    for t in twins:
        t.wait()
    for _, h in outs:
        h.wait_send()


def gather(dl, given):
    vmem = pl.BlockSpec(memory_space=pltpu.VMEM)
    dma = pltpu.SemaphoreType.DMA
    return pl.pallas_call(
        gather_kernel,
        out_shape=(
            jax.ShapeDtypeStruct((KR, 16, 128), F32),
            jax.ShapeDtypeStruct((4, 2, KD * 16, 128), F32),
        ),
        in_specs=[pl.BlockSpec(memory_space=pltpu.SMEM), vmem],
        out_specs=(vmem, vmem),
        scratch_shapes=[
            pltpu.VMEM((4, KR, 16, 128), F32),
            pltpu.VMEM((4, KR, 16, 128), F32),
            pltpu.VMEM((4, KR, 16, 128), F32),
            pltpu.VMEM((KD * 16, 128), F32),
            pltpu.VMEM((16, KD, 128), F32),
            pltpu.VMEM((KD, 128), F32),
            dma((4,)), dma((4,)), dma((4,)), dma((4,)),
            dma((16,)), dma((16,)), dma((16,)), dma((16,)),
            dma((4,)), dma((4,)), dma((4,)), dma((4,)),
        ],
        compiler_params=pltpu.CompilerParams(
            collective_id=0, has_side_effects=True, vmem_limit_bytes=32 << 20
        ),
        name="gather",
    )(dl, given.reshape(4, 2, KR, 16, 128))


def lane(x, i):
    return jnp.take_along_axis(x, jnp.full(x.shape, i, jnp.int32), axis=1)


def batched_inverse(sb, gb):
    @pl.loop(0, 16)
    def _(c):
        base = pl.multiple_of(c * 64, 64)
        e = {}
        for i in range(8):
            row = sb[pl.ds(base + i * 8, 8)]
            for k in range(i + 1):
                e[i, k] = lane(row, c * 8 + k)
        f = {}
        for k in range(8):
            f[k, k] = lax.rsqrt(e[k, k])
            for i in range(k + 1, 8):
                f[i, k] = e[i, k] * f[k, k]
            for i in range(k + 1, 8):
                for m in range(k + 1, i + 1):
                    e[i, m] = e[i, m] - f[i, k] * f[m, k]
        us, vs = [], []
        for k in range(8):
            u = sb[pl.ds(base + k * 8, 8)]
            v = gb[pl.ds(base + k * 8, 8)]
            for m in range(k):
                u = u - f[k, m] * us[m]
                v = v - f[k, m] * vs[m]
            us.append(u * f[k, k])
            vs.append(v * f[k, k])
        for k in range(8):
            gb[pl.ds(base + k * 8, 8)] = vs[k]

        @pl.loop(c + 1, 16)
        def _(q):
            low = pl.multiple_of(q * 64, 64)
            for m in range(8):
                here = pl.ds(low + m * 8, 8)
                u = sb[here]
                v = gb[here]
                for k in range(8):
                    w = lane(us[k], q * 8 + m)
                    u = u - w * us[k]
                    v = v - w * vs[k]
                sb[here] = u
                gb[here] = v


def factor_kernel(meta, x_ref, d_ref, out_ref, sb, gb, g, f, s, w, ld):
    def same(i, j):
        return meta[SAME + i * PICKS + j] > 0

    def held(value, i, j):
        return jnp.where(i // SUPER < j // SUPER, value.astype(BF16).astype(F32), value)

    def block(i, j):
        return d_ref[:, meta[POSD + i * PICKS + j]].reshape(128, 128)

    lanes = lax.broadcasted_iota(jnp.int32, (8, 128), 1)

    @pl.loop(0, meta[DEPTH])
    def _(level):
        @pl.loop(0, 128)
        def _(i):
            unit = (lanes == i).astype(F32)
            here = pl.ds(pl.multiple_of(i * 8, 8), 8)
            sb[here] = unit
            gb[here] = unit

        @pl.loop(0, PICKS)
        def _(j):
            @pl.when(meta[LEVEL + j] == level)
            def _():
                s[...] = block(j, j)

                @pl.loop(0, j)
                def _(i):
                    @pl.when(same(j, i))
                    def _():
                        w[...] = block(j, i)

                        @pl.loop(0, i)
                        def _(m):
                            @pl.when(same(j, m))
                            def _():
                                w[...] -= dot_nt(
                                    held(f[j * PICKS + m], m, i), held(f[i * PICKS + m], m, i)
                                )

                        done = dot_nt(w[...], g[i])
                        f[j * PICKS + i] = done
                        done = held(done, i, j)
                        s[...] -= dot_nt(done, done)

                sb[pl.ds(meta[FIRST + j], 128, stride=8)] = s[...]

        batched_inverse(sb, gb)

        @pl.loop(0, PICKS)
        def _(j):
            @pl.when(meta[LEVEL + j] == level)
            def _():
                g[j] = gb[pl.ds(meta[FIRST + j], 128, stride=8)]

    ld[...] = jnp.zeros_like(ld)
    out_ref[...] = jnp.zeros_like(out_ref)

    @pl.loop(0, 64)
    def _(p):
        @pl.when(meta[POS + p] >= 0)
        def _():
            a = pl.multiple_of(p // PICKS * 16, 16)
            ld[p % PICKS, pl.ds(a, 16)] = x_ref[meta[POS + p]]

    @pl.loop(0, PICKS)
    def _(j):
        @pl.loop(0, j)
        def _(i):
            @pl.when(same(j, i))
            def _():
                ld[j] -= dot_nt(held(ld[i], i, j), held(f[j * PICKS + i], i, j))

        ld[j] = dot_nt(ld[j], g[j])

    @pl.loop(0, 64)
    def _(p):
        @pl.when((meta[POS + p] >= 0) & (meta[ALIVE + p] > 0))
        def _():
            a = pl.multiple_of(p // PICKS * 16, 16)
            out_ref[meta[POS + p]] = ld[p % PICKS, pl.ds(a, 16)].astype(BF16)


def factor(meta, x, d):
    vmem = pl.BlockSpec(memory_space=pltpu.VMEM)
    return pl.pallas_call(
        factor_kernel,
        out_shape=jax.ShapeDtypeStruct((KR, 16, 128), BF16),
        in_specs=[pl.BlockSpec(memory_space=pltpu.SMEM), vmem, vmem],
        out_specs=vmem,
        scratch_shapes=[
            pltpu.VMEM((1024, 128), F32),
            pltpu.VMEM((1024, 128), F32),
            pltpu.VMEM((8, 128, 128), F32),
            pltpu.VMEM((64, 128, 128), F32),
            pltpu.VMEM((128, 128), F32),
            pltpu.VMEM((128, 128), F32),
            pltpu.VMEM((8, 128, 128), F32),
        ],
        compiler_params=pltpu.CompilerParams(vmem_limit_bytes=32 << 20),
        name="factor",
    )(meta, x, d.reshape(8, KD, 16, 128))


def share_kernel(l_ref, row_ref, col_ref, se, qe, sf, qf, sg, qg, here):
    r, c, y, k = place()
    other = {"row": r, "col": y * 2 + 1 - k}
    goal = lax.rem(r, 8)
    high = r // 8

    def along(dy):
        return {"row": r, "col": lax.rem(y + dy, 4) * 2 + k}

    barrier = pltpu.get_barrier_semaphore()
    pl.semaphore_signal(barrier, inc=1, device_id=other, device_id_type=MESH)
    for dy in (1, 2, 3):
        pl.semaphore_signal(barrier, inc=1, device_id=along(dy), device_id_type=MESH)
    for q in range(16):
        source = c + (q // 8) * 8
        far = jnp.logical_not((source == r) & (q % 8 == c))

        @pl.when(far)
        def _():
            pl.semaphore_signal(
                barrier, inc=1, device_id={"row": source, "col": q % 8}, device_id_type=MESH
            )

    pl.semaphore_wait(barrier, 19 + jnp.where(goal == c, 0, 1))

    def send(dr):
        return pltpu.make_async_remote_copy(
            src_ref=l_ref, dst_ref=col_ref.at[high, y, k],
            send_sem=sg.at[dr], recv_sem=qg.at[high * 8 + c],
            device_id={"row": lax.rem(r + dr, 16), "col": goal}, device_id_type=MESH,
        )

    for dr in range(1, 16):
        send(dr).start()
    keep = pltpu.make_async_copy(l_ref, col_ref.at[high, y, k], here.at[0])

    @pl.when(goal == c)
    def _():
        keep.start()

    @pl.when(goal != c)
    def _():
        send(0).start()

    row_ref[y, k] = l_ref[...]
    spread(row_ref, along, other, y, k, se, qe, sf, qf)

    for q in range(16):
        source = c + (q // 8) * 8
        far = jnp.logical_not((source == r) & (q % 8 == c))

        @pl.when(far)
        def _():
            pltpu.make_async_remote_copy(
                src_ref=l_ref, dst_ref=col_ref.at[q // 8, (q % 8) // 2, q % 2],
                send_sem=sg.at[0], recv_sem=qg.at[q],
                device_id=other, device_id_type=MESH,
            ).wait_recv()

    for dr in range(1, 16):
        send(dr).wait_send()

    @pl.when(goal == c)
    def _():
        keep.wait()

    @pl.when(goal != c)
    def _():
        send(0).wait_send()


def share(l):
    vmem = pl.BlockSpec(memory_space=pltpu.VMEM)
    dma = pltpu.SemaphoreType.DMA
    return pl.pallas_call(
        share_kernel,
        out_shape=(
            jax.ShapeDtypeStruct((4, 2, KR, 16, 128), BF16),
            jax.ShapeDtypeStruct((2, 4, 2, KR, 16, 128), BF16),
        ),
        in_specs=[vmem],
        out_specs=(vmem, vmem),
        scratch_shapes=[
            dma((4,)), dma((4,)), dma((4,)), dma((4,)), dma((16,)), dma((16,)), dma((1,)),
        ],
        compiler_params=pltpu.CompilerParams(
            collective_id=1, has_side_effects=True, vmem_limit_bytes=32 << 20
        ),
        name="share",
    )(l)


def update_kernel(meta, a_ref, row_ref, col_ref, panel_ref, out_ref):
    a = pl.program_id(0)
    for j in range(PICKS):
        slot = meta[POS + a * PICKS + j]
        lanes = slice((j % SUPER) * 128, (j % SUPER + 1) * 128)

        @pl.when(slot >= 0)
        def _():
            panel_ref[j // SUPER, 0, :, lanes] = row_ref[:, slot].reshape(128, 128)

        @pl.when(slot < 0)
        def _():
            panel_ref[j // SUPER, 0, :, lanes] = jnp.zeros((128, 128), BF16)

    for b in range(16):
        hit = meta[HIT + a * 16 + b] > 0

        @pl.when(hit)
        def _():
            out_ref[0, b] = a_ref[0, b]

            @pl.loop(0, PICKS)
            def _(j):
                slot = meta[POS + a * PICKS + j]

                @pl.when(slot >= 0)
                def _():
                    left = row_ref[:, slot].reshape(128, 128)
                    down = meta[POSC + (b % 2) * 64 + (b // 2) * PICKS + j]
                    right = col_ref[b % 2, :, jnp.maximum(down, 0)].reshape(128, 128)
                    out_ref[0, b] -= lax.dot_general(left, right, NT, preferred_element_type=F32)

        @pl.when(jnp.logical_not(hit))
        def _():
            out_ref[0, b] = jnp.zeros((128, 128), F32)


def update(meta, blocks, rows, cols):
    whole = lambda n: (lambda a, m: (0,) * n)
    return pl.pallas_call(
        update_kernel,
        grid_spec=pltpu.PrefetchScalarGridSpec(
            num_scalar_prefetch=1,
            grid=(8,),
            in_specs=[
                pl.BlockSpec((1, 16, 128, 128), lambda a, m: (a, 0, 0, 0)),
                pl.BlockSpec((8, KR, 16, 128), whole(4)),
                pl.BlockSpec((2, 8, KR, 16, 128), whole(5)),
            ],
            out_specs=[
                pl.BlockSpec((2, 1, 128, 512), lambda a, m: (0, a, 0, 0)),
                pl.BlockSpec((1, 16, 128, 128), lambda a, m: (a, 0, 0, 0)),
            ],
        ),
        out_shape=(
            jax.ShapeDtypeStruct((2, 8, 128, 512), BF16),
            jax.ShapeDtypeStruct((8, 16, 128, 128), F32),
        ),
        compiler_params=pltpu.CompilerParams(vmem_limit_bytes=32 << 20),
        name="update",
    )(meta, blocks, rows.reshape(8, KR, 16, 128), cols.reshape(2, 8, KR, 16, 128))


def tables(pattern, order, my_row, my_col):
    target = order[:PICKS]
    blocks = jnp.arange(128, dtype=jnp.int32)
    onehot = (target[:, None] == blocks[None, :]).astype(F32)
    linked = pattern.astype(F32)
    member = jnp.dot(onehot, linked)
    among = jnp.dot(member, onehot.T)
    index = jnp.arange(64, dtype=jnp.int32)
    before = (index[:, None] < index[None, :]).astype(F32)
    own = member.reshape(PICKS, 8, 16).transpose(2, 1, 0).reshape(16, 64)
    rank = jnp.dot(own, before)
    slot = jnp.where(own > 0, rank, -1.0)
    full = jnp.max(jnp.sum(own, axis=1))
    small = jnp.arange(PICKS)
    low = (small[None, :] <= small[:, None])
    ed = (among.T * low).reshape(1, 64)
    rankd = jnp.dot(ed, before)
    fulld = jnp.sum(ed)
    ed2 = ed.reshape(PICKS, PICKS)
    level = jnp.sum(ed2, axis=1).astype(jnp.int32) - 1
    first = jnp.min(jnp.where(ed2 > 0, small[None, :], PICKS), axis=1).astype(jnp.int32)
    by_block = slot.reshape(16, 8, PICKS).transpose(1, 0, 2).reshape(128, PICKS)
    where_d = jnp.dot(onehot, by_block)
    code = (target % 16)[:, None] * 64 + where_d.astype(jnp.int32)
    code = jnp.where(ed2 > 0, code, 0).reshape(64)
    rankd = jnp.where(ed > 0, rankd, -1.0).astype(jnp.int32).reshape(64)
    slots = jnp.arange(KD, dtype=jnp.int32)
    match = rankd[None, :] == slots[:, None]
    dl = jnp.where(
        slots < fulld.astype(jnp.int32),
        jnp.sum(jnp.where(match, code[None, :], 0), axis=1),
        16 * 64,
    )
    dead = jnp.stack([jnp.sum(onehot[:SUPER], axis=0), jnp.sum(onehot, axis=0)])
    alive = 1.0 - lax.dynamic_index_in_dim(dead.reshape(2, 8, 16), my_row, 2, keepdims=False)
    alive = jnp.repeat(alive.T, SUPER, axis=1).reshape(64).astype(jnp.int32)
    slot = slot.astype(jnp.int32)
    hit = lax.dynamic_index_in_dim(pattern.reshape(8, 16, 128), my_row, 1, keepdims=False)
    hit = lax.dynamic_index_in_dim(hit.reshape(8, 16, 8), my_col, 2, keepdims=False)
    pick_row = lambda i: lax.dynamic_index_in_dim(slot, i, 0, keepdims=False)
    meta = jnp.concatenate(
        [
            pick_row(my_row), pick_row(my_col), pick_row(my_col + 8), alive,
            ed.astype(jnp.int32).reshape(64), jnp.maximum(rankd, 0),
            target, level, first, jnp.full((8,), jnp.max(level) + 1), hit.reshape(128),
        ]
    ).astype(jnp.int32)
    fits = (full <= KR) & (fulld <= KD)
    return meta, dl.astype(jnp.int32), fits


def compact(meta, dl, blocks):
    given = pick(meta, blocks.reshape(8, 16, 8, 16, 128))
    x, d = gather(dl, given)
    l = factor(meta, x, d)
    rows, cols = share(l)
    return update(meta, blocks, rows, cols)


def broadcast(value, axis, source):
    kept = jnp.where(lax.axis_index(axis) == source, value, 0).astype(value.dtype)
    return lax.psum(kept, axis)


def dense(pattern, order, local):
    rows_axis = lax.axis_size("row")
    cols_axis = lax.axis_size("col")
    my_row = lax.axis_index("row")
    my_col = lax.axis_index("col")
    row_blocks, col_blocks, _, width = local.shape
    ratio = rows_axis // cols_axis
    total_blocks = row_blocks * rows_axis
    my_pattern = lax.dynamic_index_in_dim(
        pattern.reshape(row_blocks, rows_axis, total_blocks), my_row, 1, keepdims=False
    )
    my_pattern = lax.dynamic_index_in_dim(
        my_pattern.reshape(row_blocks, col_blocks, cols_axis), my_col, 2, keepdims=False
    )
    current = local * my_pattern.astype(F32)[:, :, None, None]
    dead = jnp.zeros((total_blocks,), F32)
    results = []
    for step in range(2):
        chosen = order[step * SUPER : (step + 1) * SUPER]
        pieces = []
        for member in range(SUPER):
            target = chosen[member]
            column_here = lax.dynamic_index_in_dim(current, target // cols_axis, 1, keepdims=False)
            pieces.append(broadcast(column_here, "col", target % cols_axis))
        panel = jnp.concatenate(pieces, axis=2)
        parts_list = []
        for member in range(SUPER):
            target = chosen[member]
            row_here = lax.dynamic_index_in_dim(panel, target // rows_axis, 0, keepdims=False)
            parts_list.append(
                jnp.where(target % rows_axis == my_row, row_here, jnp.zeros_like(row_here))
            )
        square = lax.psum(jnp.concatenate(parts_list, axis=0), "row")
        factored = jnp.linalg.cholesky(square)
        flat = panel.reshape(row_blocks * width, SUPER * width)
        lower = lax.linalg.triangular_solve(
            factored, flat, left_side=False, lower=True, transpose_a=True
        )
        dead = dead.at[chosen].set(1.0)
        alive = lax.dynamic_index_in_dim(
            (1.0 - dead).reshape(row_blocks, rows_axis), my_row, 1, keepdims=False
        )
        rounded = (lower.reshape(row_blocks, width, SUPER * width) * alive[:, None, None]).astype(
            BF16
        )
        results.append(rounded)
        whole = lax.all_gather(rounded, "row", axis=0, tiled=True)
        whole = whole.reshape(ratio, cols_axis, row_blocks, width, SUPER * width)
        picked = lax.dynamic_index_in_dim(whole, my_col, 1, keepdims=False)
        column_panel = picked.transpose(1, 0, 2, 3).reshape(col_blocks, width, SUPER * width)
        change = jnp.einsum("aik,cjk->acij", rounded, column_panel, preferred_element_type=F32)
        current = current - change
    return jnp.stack(results), current


def shards(matrix_blocks, pattern, order):
    local = matrix_blocks[:, 0, :, 0]
    meta, dl, fits = tables(pattern, order, lax.axis_index("row"), lax.axis_index("col"))
    panels, trailing = lax.cond(
        fits,
        lambda: compact(meta, dl, local),
        lambda: dense(pattern, order, local),
    )
    return panels[:, :, None], trailing[:, None, :, None]


def solution(mesh):
    in_specs = (P(None, "row", None, "col", None, None), P(), P())
    out_specs = (P(None, None, "row", None, None), P(None, "row", None, "col", None, None))
    return jax.shard_map(shards, mesh=mesh, in_specs=in_specs, out_specs=out_specs, check_vma=False)
```

time: 967 us -> 195 us (0.20)
  waiting for transfers between devices: 517 us -> 0 us
  other arithmetic: 266 us -> 2.56 us
  Pallas kernels: 0 us -> 167 us
  local copies, waits for them, and re-layouts: 91.5 us -> 2.58 us
  matrix products: 46.4 us -> 2.31 us
  between operations: 40.6 us -> 16.7 us
    psum x4 -> x0, waiting for transfers between devices: 297 us -> none  [the longest x2 166 us: shards(): square = lax.psum(jnp.concatenate(parts_list, axis=0), 'row')]
    another operation x34 -> x0, other arithmetic: 240 us -> none  [the longest x29 158 us: shards(): factor = jnp.linalg.cholesky(square)]
    all_gather x2 -> x0, waiting for transfers between devices: 220 us -> none  [shards(): whole = lax.all_gather(rounded, 'row', axis=0, tiled=True)]
    pallas_call x0 -> x5, Pallas kernels: none -> 167 us  [the longest x1 59.3 us: factor(): pl.pallas_call(factor_kernel, out_shape=jax.ShapeDtypeStruct((KR, 16, 128...]
    another operation x26 -> x0, matrix products: 33.9 us -> none  [the longest x14 23 us: shards(): lax.linalg.triangular_solve(factor, flat, left_side=False, lower=True, tr...]
    unnamed x50 -> x0, local copies, waits for them, and re-layouts: 33 us -> none
    another operation x36 -> x4, local copies, waits for them, and re-layouts: 23.4 us -> 0.25 us  [the longest x2 0.16 us: tables(): dead = jnp.stack([jnp.sum(onehot[:SUPER], axis=0), jnp.sum(onehot, axis=0)])]
    dynamic_slice x7 -> x2, local copies, waits for them, and re-layouts: 14.5 us -> 1.06 us  [the longest x1 0.77 us: tables(): lax.dynamic_index_in_dim(pattern.reshape(8, 16, 128), my_row, 1, keepdims...]
  transfers between devices with their start and end apart: 6 -> 0, of which waited for: 6 -> 0; matrix products, arithmetic and copies ran while one was open for 2% -> 0% of each run, Pallas kernels for 0% -> 0%
where the time goes in v1:
time: 195 us; the launch traced here: 192 us
  Pallas kernels  167 us (86%)
  between operations  16.7 us (9%)
  local copies, waits for them, and re-layouts  2.58 us (1%)
  other arithmetic  2.56 us (1%)
  matrix products  2.31 us (1%)
    pallas_call x1, Pallas kernels, factor(): pl.pallas_call(factor_kernel, out_shape=jax.ShapeDtypeStruct((KR, 16, 128...  59.3 us
    pallas_call x1, Pallas kernels, share(): pl.pallas_call(share_kernel, out_shape=(jax.ShapeDtypeStruct((4, 2, KR, 1...  54 us
    pallas_call x1, Pallas kernels, gather(): pl.pallas_call(gather_kernel, out_shape=(jax.ShapeDtypeStruct((KR, 16, 12...  42 us
    pallas_call x1, Pallas kernels, update(): pl.pallas_call(update_kernel, grid_spec=pltpu.PrefetchScalarGridSpec(num_...  8.84 us

profile of v1, /device:TPU:3, one launch (start us, length us, event | category | flops | bytes accessed | tf_op | source)
XLA Modules:
  0.0 191.9 jit_solution(15119500266270076888)
XLA Ops:
  7.2 0.7 compare_select_fusion.3
  8.2 0.2 fusion.87
  8.4 0.1 copy.88
  8.6 0.1 convert_element_type.106
  8.7 0.8 constant_dynamic-slice_fusion.7
  9.4 1.0 fusion.102
  10.6 0.6 reduce_max.18
  11.8 0.8 fusion.98
  13.9 0.6 fusion.97
  15.5 0.1 broadcast_maximum_fusion
  15.8 0.2 fusion.103
  16.0 0.1 copy.91
  16.1 0.1 reshape.242
  16.2 0.2 convolution_convert_fusion
  16.4 0.1 reshape.239
  16.5 0.3 dynamic-slice_reduce_fusion
  16.9 168.2 %conditional.1 = (bf16[2,8,1,128,512]{4,3,2,1,0:T(8,128)(2,1)}, f32[8,1,16,1,128,128]{5,4,3,2,1,0:T(8,128)}) conditional(s32[]{:T(128)} %convert_element_type.100, (s32[128]{0:T(128)}, s32[128,128]{1,0:T(8,128)}, f32[8,16,128,128]{3,2,1,0:T(8,128)}) %tuple.170, (f32[8,1,16,1,128,128]{5,4,3,2,1,0:T(8,128)}, s32[544]{0:T(1024)S(1)}, ...), branch_computations={%region_10.33_spmd, %region_31.34_spmd} | conditional | flops 9155118080 | bytes 515429952 | solution.py:656
  17.2 0.1 copy.95
  17.4 0.1 select_reduce_fusion
  17.6 3.3 %pick.1 = f32[8,24,16,128]{3,2,1,0:T(8,128)S(1)} custom-call(s32[544]{0:T(1024)S(1)} %get-tuple-element.23.meta, f32[8,16,8,16,128]{4,3,2,1,0:T(8,128)} %bitcast.276), custom_call_target="tpu_custom_call" | custom-call | tf_op jit(solution)/shard_map/cond/branch_1_fun/pick/pallas_call | solution.py:66
  20.9 42.0 %gather.4 = (f32[24,16,128]{2,1,0:T(8,128)S(1)}, f32[4,2,384,128]{3,2,1,0:T(8,128)S(1)}) custom-call(s32[24]{0:T(128)S(1)} %compare_select_fusion.dl_ref, f32[4,2,24,16,128]{4,3,2,1,0:T(8,128)S(1)} %bitcast.270), custom_call_target="tpu_custom_call" | custom-call | tf_op jit(solution)/shard_map/cond/branch_1_fun/gather/pallas_call | solution.py:200
  62.9 59.3 %factor.1.l_ref = bf16[24,16,128]{2,1,0:T(8,128)(2,1)S(1)} custom-call(s32[544]{0:T(1024)S(1)} %get-tuple-element.23.meta, f32[24,16,128]{2,1,0:T(8,128)S(1)} %get-tuple-element.27.x_ref, f32[8,24,16,128]{3,2,1,0:T(8,128)S(1)} %bitcast.272), custom_call_target="tpu_custom_call" | custom-call | tf_op jit(solution)/shard_map/cond/branch_1_fun/factor/pallas_call | solution.py:360
  122.2 54.0 %share.1 = (bf16[4,2,24,16,128]{4,3,2,1,0:T(8,128)(2,1)S(1)}, bf16[2,4,2,24,16,128]{5,4,3,2,1,0:T(8,128)(2,1)S(1)}) custom-call(bf16[24,16,128]{2,1,0:T(8,128)(2,1)S(1)} %factor.1.l_ref), custom_call_target="tpu_custom_call" | custom-call | tf_op jit(solution)/shard_map/cond/branch_1_fun/share/pallas_call | solution.py:453
  176.2 8.8 %update.1 = (bf16[2,8,128,512]{3,2,1,0:T(8,128)(2,1)}, f32[8,16,128,128]{3,2,1,0:T(8,128)}) custom-call(s32[544]{0:T(1024)S(1)} %get-tuple-element.23.meta, f32[8,16,128,128]{3,2,1,0:T(8,128)S(1)} %copy-done, bf16[8,24,16,128]{3,2,1,0:T(8,128)(2,1)S(1)} %bitcast.273, bf16[2,8,24,16,128]{4,3,2,1,0:T(8,128)(2,1)S(1)} %bitcast.271), custom_call_target="tpu_custom_call" | custom-call | tf_op jit(solution)/shard_map/cond/branch_1_fun/update/pallas_call | solution.py:510
  (30 shorter events, 1.3 us)
Async XLA Ops:
  17.5 158.7 %copy-start = (f32[8,16,128,128]{3,2,1,0:T(8,128)S(1)}, f32[8,16,128,128]{3,2,1,0:T(8,128)}, u32[]{:S(2)}) copy-start(f32[8,16,128,128]{3,2,1,0:T(8,128)} %get-tuple-element.24.a_ref) | copy-start | bytes 25165828 | tf_op jit(solution)/shard_map/cond

commit v2 on v1

--- a/solution.py
+++ b/solution.py
@@ -4,13 +4,14 @@
 import jax.numpy as jnp
 from jax import lax
 from jax.experimental import pallas as pl
+from jax.experimental.layout import Layout, with_layout_constraint
 from jax.experimental.pallas import tpu as pltpu
 from jax.sharding import PartitionSpec as P
 
 SUPER = 4
+GROUP = 4
 PICKS = 8
-KR = 24
-KD = 24
+TIERS = (16, 32)
 MESH = pl.DeviceIdType.MESH
 HIGH = lax.Precision.HIGHEST
 F32 = jnp.float32
@@ -24,9 +25,10 @@
 POSD = 320
 TARGET = 384
 LEVEL = 392
-FIRST = 400
-DEPTH = 408
-HIT = 416
+PLACE = 400
+COUNT = 408
+DEPTH = 416
+HIT = 424
 
 
 def dot_nt(a, b):
@@ -62,13 +64,13 @@
             c.wait()
 
 
-def pick(meta, blocks):
+def pick(slots, meta, blocks):
     return pl.pallas_call(
         pick_kernel,
-        out_shape=jax.ShapeDtypeStruct((8, KR, 16, 128), F32),
+        out_shape=jax.ShapeDtypeStruct((8, slots, 16, 128), F32),
         in_specs=[pl.BlockSpec(memory_space=pltpu.SMEM), pl.BlockSpec(memory_space=pl.ANY)],
         out_specs=pl.BlockSpec(memory_space=pltpu.VMEM),
-        scratch_shapes=[pltpu.SemaphoreType.DMA((KR,))],
+        scratch_shapes=[pltpu.SemaphoreType.DMA((slots,))],
         compiler_params=pltpu.CompilerParams(vmem_limit_bytes=16 << 20),
         name="pick",
     )(meta, blocks)
@@ -84,6 +86,7 @@
     dl_ref, give_ref, x_ref, d_ref, ra, acc, rb, dsrc, rr, piece,
     sa, qa, sb, qb, sc, qc, sd, qd, se, qe, sf, qf,
 ):
+    slots = x_ref.shape[0]
     r, c, y, k = place()
     other = {"row": r, "col": y * 2 + 1 - k}
 
@@ -128,7 +131,7 @@
         total = total + rb[dy]
     x_ref[...] = total
 
-    for d in range(KD):
+    for d in range(slots):
         code = dl_ref[d]
         mine = (code // 64 == r).astype(F32)
         dsrc[d * 16 : (d + 1) * 16] = x_ref[code % 64] * mine
@@ -136,17 +139,17 @@
     for dr in range(1, 16):
         there = lax.rem(r + dr, 16)
         h = pltpu.make_async_remote_copy(
-            src_ref=dsrc.at[pl.ds(there * KD, KD)], dst_ref=rr.at[dr],
+            src_ref=dsrc.at[pl.ds(there * slots, slots)], dst_ref=rr.at[dr],
             send_sem=sc.at[dr], recv_sem=qc.at[dr], device_id=across(dr), device_id_type=MESH,
         )
         h.start()
         parts.append(h)
-    total = dsrc[pl.ds(pl.multiple_of(r * KD, 8), KD)]
+    total = dsrc[pl.ds(pl.multiple_of(r * slots, 8), slots)]
     for dr, h in zip(range(1, 16), parts):
         h.wait_recv()
         total = total + rr[dr]
     piece[...] = total
-    mine = pl.ds(pl.multiple_of(r * KD, 8), KD)
+    mine = pl.ds(pl.multiple_of(r * slots, 8), slots)
     d_ref[y, k, mine] = total
     wholes = []
     for dr in range(1, 16):
@@ -195,83 +198,111 @@
 
 
 def gather(dl, given):
+    slots = given.shape[1]
     vmem = pl.BlockSpec(memory_space=pltpu.VMEM)
     dma = pltpu.SemaphoreType.DMA
     return pl.pallas_call(
         gather_kernel,
         out_shape=(
-            jax.ShapeDtypeStruct((KR, 16, 128), F32),
-            jax.ShapeDtypeStruct((4, 2, KD * 16, 128), F32),
+            jax.ShapeDtypeStruct((slots, 16, 128), F32),
+            jax.ShapeDtypeStruct((4, 2, slots * 16, 128), F32),
         ),
         in_specs=[pl.BlockSpec(memory_space=pltpu.SMEM), vmem],
         out_specs=(vmem, vmem),
         scratch_shapes=[
-            pltpu.VMEM((4, KR, 16, 128), F32),
-            pltpu.VMEM((4, KR, 16, 128), F32),
-            pltpu.VMEM((4, KR, 16, 128), F32),
-            pltpu.VMEM((KD * 16, 128), F32),
-            pltpu.VMEM((16, KD, 128), F32),
-            pltpu.VMEM((KD, 128), F32),
+            pltpu.VMEM((4, slots, 16, 128), F32),
+            pltpu.VMEM((4, slots, 16, 128), F32),
+            pltpu.VMEM((4, slots, 16, 128), F32),
+            pltpu.VMEM((slots * 16, 128), F32),
+            pltpu.VMEM((16, slots, 128), F32),
+            pltpu.VMEM((slots, 128), F32),
             dma((4,)), dma((4,)), dma((4,)), dma((4,)),
             dma((16,)), dma((16,)), dma((16,)), dma((16,)),
             dma((4,)), dma((4,)), dma((4,)), dma((4,)),
         ],
         compiler_params=pltpu.CompilerParams(
-            collective_id=0, has_side_effects=True, vmem_limit_bytes=32 << 20
+            collective_id=slots, has_side_effects=True, vmem_limit_bytes=32 << 20
         ),
         name="gather",
-    )(dl, given.reshape(4, 2, KR, 16, 128))
+    )(dl, given.reshape(4, 2, slots, 16, 128))
 
 
 def lane(x, i):
     return jnp.take_along_axis(x, jnp.full(x.shape, i, jnp.int32), axis=1)
 
 
-def batched_inverse(sb, gb):
-    @pl.loop(0, 16)
+def pivots(us, vs, first):
+    e = {}
+    for i in range(8):
+        for k in range(i + 1):
+            e[i, k] = lane(us[i], first + k)
+    f = {}
+    for k in range(8):
+        f[k, k] = lax.rsqrt(e[k, k])
+        for i in range(k + 1, 8):
+            f[i, k] = e[i, k] * f[k, k]
+        for i in range(k + 1, 8):
+            for m in range(k + 1, i + 1):
+                e[i, m] = e[i, m] - f[i, k] * f[m, k]
+    outs, outv = [], []
+    for k in range(8):
+        u, v = us[k], vs[k]
+        for m in range(k):
+            u = u - f[k, m] * outs[m]
+            v = v - f[k, m] * outv[m]
+        outs.append(u * f[k, k])
+        outv.append(v * f[k, k])
+    return outs, outv
+
+
+def split(x):
+    high = x.astype(BF16)
+    x = x - high.astype(F32)
+    middle = x.astype(BF16)
+    return high, middle, (x - middle.astype(F32)).astype(BF16)
+
+
+def batched_inverse(st, ht, ub, vb, count):
+    lanes = lax.broadcasted_iota(jnp.int32, (16, 128), 1)
+
+    @pl.loop(0, 8)
     def _(c):
-        base = pl.multiple_of(c * 64, 64)
-        e = {}
-        for i in range(8):
-            row = sb[pl.ds(base + i * 8, 8)]
-            for k in range(i + 1):
-                e[i, k] = lane(row, c * 8 + k)
-        f = {}
-        for k in range(8):
-            f[k, k] = lax.rsqrt(e[k, k])
-            for i in range(k + 1, 8):
-                f[i, k] = e[i, k] * f[k, k]
-            for i in range(k + 1, 8):
-                for m in range(k + 1, i + 1):
-                    e[i, m] = e[i, m] - f[i, k] * f[m, k]
-        us, vs = [], []
-        for k in range(8):
-            u = sb[pl.ds(base + k * 8, 8)]
-            v = gb[pl.ds(base + k * 8, 8)]
-            for m in range(k):
-                u = u - f[k, m] * us[m]
-                v = v - f[k, m] * vs[m]
-            us.append(u * f[k, k])
-            vs.append(v * f[k, k])
-        for k in range(8):
-            gb[pl.ds(base + k * 8, 8)] = vs[k]
-
-        @pl.loop(c + 1, 16)
-        def _(q):
-            low = pl.multiple_of(q * 64, 64)
-            for m in range(8):
-                here = pl.ds(low + m * 8, 8)
-                u = sb[here]
-                v = gb[here]
-                for k in range(8):
-                    w = lane(us[k], q * 8 + m)
-                    u = u - w * us[k]
-                    v = v - w * vs[k]
-                sb[here] = u
-                gb[here] = v
-
-
-def factor_kernel(meta, x_ref, d_ref, out_ref, sb, gb, g, f, s, w, ld):
+        base = c * 16
+        us = [st[pl.ds(base + k, 8, stride=128)] for k in range(16)]
+        vs = [ht[pl.ds(base + k, 8, stride=128)] for k in range(16)]
+        us[:8], vs[:8] = pivots(us[:8], vs[:8], base)
+        for m in range(8, 16):
+            for k in range(8):
+                w = lane(us[k], base + m)
+                us[m] = us[m] - w * us[k]
+                vs[m] = vs[m] - w * vs[k]
+        us[8:], vs[8:] = pivots(us[8:], vs[8:], base + 8)
+        for k in range(16):
+            ht[pl.ds(base + k, 8, stride=128)] = vs[k]
+            ub[pl.ds(k, 8, stride=16)] = us[k]
+            vb[pl.ds(k, 8, stride=16)] = vs[k]
+
+        @pl.when(c < 7)
+        def _():
+            @pl.loop(0, (count + GROUP - 1) // GROUP)
+            def _(q):
+                for t in range(GROUP):
+                    b = q * GROUP + t
+                    here = pl.ds(pl.multiple_of(b * 16, 16), 16)
+                    u = ub[here]
+                    x, y, z = split(jnp.where(lanes >= base + 16, u, 0.0))
+                    left = jnp.concatenate([x, x, y, y, x, z], axis=0)
+                    x, y, z = split(jnp.concatenate([u, vb[here]], axis=1))
+                    right = jnp.concatenate([x, y, x, y, z, x], axis=0)
+                    change = lax.dot_general(
+                        left, right, (((0,), (0,)), ((), ())), preferred_element_type=F32
+                    )
+                    rows = pl.ds(pl.multiple_of(b * 128, 128), 128)
+                    st[rows] -= change[:, :128]
+                    ht[rows] -= change[:, 128:]
+
+
+def factor_kernel(meta, x_ref, d_ref, out_ref, st, ht, ub, vb, g, f, s, w, ld):
     def same(i, j):
         return meta[SAME + i * PICKS + j] > 0
 
@@ -281,16 +312,15 @@
     def block(i, j):
         return d_ref[:, meta[POSD + i * PICKS + j]].reshape(128, 128)
 
-    lanes = lax.broadcasted_iota(jnp.int32, (8, 128), 1)
+    st[...] = jnp.zeros_like(st)
+    unit = lax.broadcasted_iota(jnp.int32, (128, 128), 0) == lax.broadcasted_iota(
+        jnp.int32, (128, 128), 1
+    )
 
     @pl.loop(0, meta[DEPTH])
     def _(level):
-        @pl.loop(0, 128)
-        def _(i):
-            unit = (lanes == i).astype(F32)
-            here = pl.ds(pl.multiple_of(i * 8, 8), 8)
-            sb[here] = unit
-            gb[here] = unit
+        for b in range(8):
+            ht[b * 128 : (b + 1) * 128] = unit.astype(F32)
 
         @pl.loop(0, PICKS)
         def _(j):
@@ -317,15 +347,15 @@
                         done = held(done, i, j)
                         s[...] -= dot_nt(done, done)
 
-                sb[pl.ds(meta[FIRST + j], 128, stride=8)] = s[...]
-
-        batched_inverse(sb, gb)
+                st[pl.ds(pl.multiple_of(meta[PLACE + j] * 128, 128), 128)] = s[...]
+
+        batched_inverse(st, ht, ub, vb, meta[COUNT + level])
 
         @pl.loop(0, PICKS)
         def _(j):
             @pl.when(meta[LEVEL + j] == level)
             def _():
-                g[j] = gb[pl.ds(meta[FIRST + j], 128, stride=8)]
+                g[j] = ht[pl.ds(pl.multiple_of(meta[PLACE + j] * 128, 128), 128)]
 
     ld[...] = jnp.zeros_like(ld)
     out_ref[...] = jnp.zeros_like(out_ref)
@@ -356,15 +386,18 @@
 
 
 def factor(meta, x, d):
+    slots = x.shape[0]
     vmem = pl.BlockSpec(memory_space=pltpu.VMEM)
     return pl.pallas_call(
         factor_kernel,
-        out_shape=jax.ShapeDtypeStruct((KR, 16, 128), BF16),
+        out_shape=jax.ShapeDtypeStruct((slots, 16, 128), BF16),
         in_specs=[pl.BlockSpec(memory_space=pltpu.SMEM), vmem, vmem],
         out_specs=vmem,
         scratch_shapes=[
             pltpu.VMEM((1024, 128), F32),
             pltpu.VMEM((1024, 128), F32),
+            pltpu.VMEM((128, 128), F32),
+            pltpu.VMEM((128, 128), F32),
             pltpu.VMEM((8, 128, 128), F32),
             pltpu.VMEM((64, 128, 128), F32),
             pltpu.VMEM((128, 128), F32),
@@ -373,11 +406,13 @@
         ],
         compiler_params=pltpu.CompilerParams(vmem_limit_bytes=32 << 20),
         name="factor",
-    )(meta, x, d.reshape(8, KD, 16, 128))
-
-
-def share_kernel(l_ref, row_ref, col_ref, se, qe, sf, qf, sg, qg, here):
+    )(meta, x, d.reshape(8, slots, 16, 128))
+
+
+def share_kernel(l_ref, row_ref, col_ref, se, qe, sf, qf, sg, qg, sx, qx, sz, qz):
+    n = l_ref.shape[0] // 16
     r, c, y, k = place()
+    z, x = r // 4, lax.rem(r, 4)
     other = {"row": r, "col": y * 2 + 1 - k}
     goal = lax.rem(r, 8)
     high = r // 8
@@ -385,62 +420,106 @@
     def along(dy):
         return {"row": r, "col": lax.rem(y + dy, 4) * 2 + k}
 
+    def along_x(d):
+        return {"row": z * 4 + lax.rem(x + d, 4), "col": c}
+
+    def along_z(d):
+        return {"row": lax.rem(z + d, 4) * 4 + x, "col": c}
+
+    def greet(device):
+        pl.semaphore_signal(barrier, inc=1, device_id=device, device_id_type=MESH)
+
     barrier = pltpu.get_barrier_semaphore()
-    pl.semaphore_signal(barrier, inc=1, device_id=other, device_id_type=MESH)
-    for dy in (1, 2, 3):
-        pl.semaphore_signal(barrier, inc=1, device_id=along(dy), device_id_type=MESH)
+    greet(other)
+    for d in (1, 2, 3):
+        greet(along(d))
+        greet(along_x(d))
+        greet(along_z(d))
     for q in range(16):
         source = c + (q // 8) * 8
         far = jnp.logical_not((source == r) & (q % 8 == c))
 
         @pl.when(far)
         def _():
-            pl.semaphore_signal(
-                barrier, inc=1, device_id={"row": source, "col": q % 8}, device_id_type=MESH
-            )
-
-    pl.semaphore_wait(barrier, 19 + jnp.where(goal == c, 0, 1))
-
-    def send(dr):
+            greet({"row": source, "col": q % 8})
+
+    pl.semaphore_wait(barrier, 25 + jnp.where(goal == c, 0, 1))
+
+    def send(d):
+        m = lax.rem(r + d, 16)
         return pltpu.make_async_remote_copy(
-            src_ref=l_ref, dst_ref=col_ref.at[high, y, k],
-            send_sem=sg.at[dr], recv_sem=qg.at[high * 8 + c],
-            device_id={"row": lax.rem(r + dr, 16), "col": goal}, device_id_type=MESH,
-        )
-
-    for dr in range(1, 16):
-        send(dr).start()
-    keep = pltpu.make_async_copy(l_ref, col_ref.at[high, y, k], here.at[0])
+            src_ref=l_ref.at[pl.ds(m * n, n)],
+            dst_ref=col_ref.at[high, m // 4, lax.rem(m, 4), :, c],
+            send_sem=sg.at[d], recv_sem=qg.at[high * 8 + c],
+            device_id={"row": m, "col": goal}, device_id_type=MESH,
+        )
+
+    for d in range(1, 16):
+        send(d).start()
 
     @pl.when(goal == c)
     def _():
-        keep.start()
+        col_ref[high, z, x, :, c] = l_ref[pl.ds(r * n, n)]
 
     @pl.when(goal != c)
     def _():
         send(0).start()
 
     row_ref[y, k] = l_ref[...]
-    spread(row_ref, along, other, y, k, se, qe, sf, qf)
-
-    for q in range(16):
-        source = c + (q // 8) * 8
-        far = jnp.logical_not((source == r) & (q % 8 == c))
-
-        @pl.when(far)
-        def _():
-            pltpu.make_async_remote_copy(
-                src_ref=l_ref, dst_ref=col_ref.at[q // 8, (q % 8) // 2, q % 2],
-                send_sem=sg.at[0], recv_sem=qg.at[q],
-                device_id=other, device_id_type=MESH,
-            ).wait_recv()
-
-    for dr in range(1, 16):
-        send(dr).wait_send()
-
-    @pl.when(goal == c)
-    def _():
-        keep.wait()
+    outs = []
+    for d in (2, 1, 3):
+        h = pltpu.make_async_remote_copy(
+            src_ref=row_ref.at[y, k], dst_ref=row_ref.at[y, k],
+            send_sem=se.at[d], recv_sem=qe.at[d], device_id=along(d), device_id_type=MESH,
+        )
+        h.start()
+        outs.append((d, h))
+
+    def move(ref, s, q, device):
+        h = pltpu.make_async_remote_copy(
+            src_ref=ref, dst_ref=ref, send_sem=s, recv_sem=q, device_id=device, device_id_type=MESH
+        )
+        h.start()
+        return h
+
+    near = []
+    for half in range(2):
+        for q in range(half * 8, half * 8 + 8):
+            far = jnp.logical_not((c + half * 8 == r) & (q % 8 == c))
+
+            @pl.when(far)
+            def _():
+                pltpu.make_async_remote_copy(
+                    src_ref=l_ref.at[pl.ds(0, n)], dst_ref=col_ref.at[half, z, x, :, q % 8],
+                    send_sem=sg.at[0], recv_sem=qg.at[q], device_id=other, device_id_type=MESH,
+                ).wait_recv()
+
+        for d in (2, 1, 3):
+            if half == 0:
+                near.append(move(col_ref.at[0, z, x], sx.at[d], qx.at[d], along_x(d)))
+            else:
+                near.append(move(col_ref.at[1, z, x], sz.at[d], qz.at[d], along_z(d)))
+
+    twins = []
+    for d in (0, 1, 3, 2):
+        come = lax.rem(y + 4 - d, 4)
+        for e, h in outs:
+            if e == d:
+                h.wait_recv()
+        twins.append(move(row_ref.at[come, k], sf.at[d], qf.at[d], other))
+
+    for h in near:
+        h.wait_recv()
+    last = []
+    for d in (2, 1, 3):
+        last.append(move(col_ref.at[0, z], sx.at[3 + d], qx.at[3 + d], along_z(d)))
+        last.append(move(col_ref.at[1, :, x], sz.at[3 + d], qz.at[3 + d], along_x(d)))
+    for h in twins + last:
+        h.wait()
+    for h in near + [h for _, h in outs]:
+        h.wait_send()
+    for d in range(1, 16):
+        send(d).wait_send()
 
     @pl.when(goal != c)
     def _():
@@ -448,21 +527,23 @@
 
 
 def share(l):
+    slots = l.shape[0]
     vmem = pl.BlockSpec(memory_space=pltpu.VMEM)
     dma = pltpu.SemaphoreType.DMA
     return pl.pallas_call(
         share_kernel,
         out_shape=(
-            jax.ShapeDtypeStruct((4, 2, KR, 16, 128), BF16),
-            jax.ShapeDtypeStruct((2, 4, 2, KR, 16, 128), BF16),
+            jax.ShapeDtypeStruct((4, 2, slots, 16, 128), BF16),
+            jax.ShapeDtypeStruct((2, 4, 4, slots // 16, 8, 16, 128), BF16),
         ),
         in_specs=[vmem],
         out_specs=(vmem, vmem),
         scratch_shapes=[
-            dma((4,)), dma((4,)), dma((4,)), dma((4,)), dma((16,)), dma((16,)), dma((1,)),
+            dma((4,)), dma((4,)), dma((4,)), dma((4,)), dma((16,)), dma((16,)),
+            dma((7,)), dma((7,)), dma((7,)), dma((7,)),
         ],
         compiler_params=pltpu.CompilerParams(
-            collective_id=1, has_side_effects=True, vmem_limit_bytes=32 << 20
+            collective_id=slots + 1, has_side_effects=True, vmem_limit_bytes=32 << 20
         ),
         name="share",
     )(l)
@@ -497,7 +578,7 @@
                 def _():
                     left = row_ref[:, slot].reshape(128, 128)
                     down = meta[POSC + (b % 2) * 64 + (b // 2) * PICKS + j]
-                    right = col_ref[b % 2, :, jnp.maximum(down, 0)].reshape(128, 128)
+                    right = col_ref[b % 2, jnp.maximum(down, 0)]
                     out_ref[0, b] -= lax.dot_general(left, right, NT, preferred_element_type=F32)
 
         @pl.when(jnp.logical_not(hit))
@@ -506,6 +587,7 @@
 
 
 def update(meta, blocks, rows, cols):
+    slots = rows.shape[2]
     whole = lambda n: (lambda a, m: (0,) * n)
     return pl.pallas_call(
         update_kernel,
@@ -514,8 +596,8 @@
             grid=(8,),
             in_specs=[
                 pl.BlockSpec((1, 16, 128, 128), lambda a, m: (a, 0, 0, 0)),
-                pl.BlockSpec((8, KR, 16, 128), whole(4)),
-                pl.BlockSpec((2, 8, KR, 16, 128), whole(5)),
+                pl.BlockSpec((8, slots, 16, 128), whole(4)),
+                pl.BlockSpec((2, slots, 128, 128), whole(4)),
             ],
             out_specs=[
                 pl.BlockSpec((2, 1, 128, 512), lambda a, m: (0, a, 0, 0)),
@@ -528,7 +610,7 @@
         ),
         compiler_params=pltpu.CompilerParams(vmem_limit_bytes=32 << 20),
         name="update",
-    )(meta, blocks, rows.reshape(8, KR, 16, 128), cols.reshape(2, 8, KR, 16, 128))
+    )(meta, blocks, rows.reshape(8, slots, 16, 128), cols.reshape(2, slots, 128, 128))
 
 
 def tables(pattern, order, my_row, my_col):
@@ -551,13 +633,15 @@
     fulld = jnp.sum(ed)
     ed2 = ed.reshape(PICKS, PICKS)
     level = jnp.sum(ed2, axis=1).astype(jnp.int32) - 1
-    first = jnp.min(jnp.where(ed2 > 0, small[None, :], PICKS), axis=1).astype(jnp.int32)
+    peers = level[:, None] == level[None, :]
+    spot = jnp.sum(peers & (small[None, :] < small[:, None]), axis=1)
+    count = jnp.sum(level[None, :] == small[:, None], axis=1)
     by_block = slot.reshape(16, 8, PICKS).transpose(1, 0, 2).reshape(128, PICKS)
     where_d = jnp.dot(onehot, by_block)
     code = (target % 16)[:, None] * 64 + where_d.astype(jnp.int32)
     code = jnp.where(ed2 > 0, code, 0).reshape(64)
     rankd = jnp.where(ed > 0, rankd, -1.0).astype(jnp.int32).reshape(64)
-    slots = jnp.arange(KD, dtype=jnp.int32)
+    slots = jnp.arange(TIERS[-1], dtype=jnp.int32)
     match = rankd[None, :] == slots[:, None]
     dl = jnp.where(
         slots < fulld.astype(jnp.int32),
@@ -575,16 +659,17 @@
         [
             pick_row(my_row), pick_row(my_col), pick_row(my_col + 8), alive,
             ed.astype(jnp.int32).reshape(64), jnp.maximum(rankd, 0),
-            target, level, first, jnp.full((8,), jnp.max(level) + 1), hit.reshape(128),
+            target, level, spot, count, jnp.full((8,), jnp.max(level) + 1), hit.reshape(128),
         ]
     ).astype(jnp.int32)
-    fits = (full <= KR) & (fulld <= KD)
-    return meta, dl.astype(jnp.int32), fits
-
-
-def compact(meta, dl, blocks):
-    given = pick(meta, blocks.reshape(8, 16, 8, 16, 128))
-    x, d = gather(dl, given)
+    need = jnp.maximum(full, fulld)
+    tier = sum((need > slots).astype(jnp.int32) for slots in TIERS)
+    return meta, dl.astype(jnp.int32), tier
+
+
+def compact(slots, meta, dl, blocks):
+    given = pick(slots, meta, blocks.reshape(8, 16, 8, 16, 128))
+    x, d = gather(dl[:slots], given)
     l = factor(meta, x, d)
     rows, cols = share(l)
     return update(meta, blocks, rows, cols)
@@ -601,6 +686,7 @@
     my_row = lax.axis_index("row")
     my_col = lax.axis_index("col")
     row_blocks, col_blocks, _, width = local.shape
+    local = with_layout_constraint(local, Layout((0, 1, 2, 3)))
     ratio = rows_axis // cols_axis
     total_blocks = row_blocks * rows_axis
     my_pattern = lax.dynamic_index_in_dim(
@@ -647,17 +733,15 @@
         column_panel = picked.transpose(1, 0, 2, 3).reshape(col_blocks, width, SUPER * width)
         change = jnp.einsum("aik,cjk->acij", rounded, column_panel, preferred_element_type=F32)
         current = current - change
-    return jnp.stack(results), current
+    panels = with_layout_constraint(jnp.stack(results), Layout((0, 1, 2, 3)))
+    return panels, with_layout_constraint(current, Layout((0, 1, 2, 3)))
 
 
 def shards(matrix_blocks, pattern, order):
     local = matrix_blocks[:, 0, :, 0]
-    meta, dl, fits = tables(pattern, order, lax.axis_index("row"), lax.axis_index("col"))
-    panels, trailing = lax.cond(
-        fits,
-        lambda: compact(meta, dl, local),
-        lambda: dense(pattern, order, local),
-    )
+    meta, dl, tier = tables(pattern, order, lax.axis_index("row"), lax.axis_index("col"))
+    ways = [functools.partial(compact, slots, meta, dl, local) for slots in TIERS]
+    panels, trailing = lax.switch(tier, ways + [lambda: dense(pattern, order, local)])
     return panels[:, :, None], trailing[:, None, :, None]
 
 

time: 195 us -> 129 us (0.66); the launches traced: 192 us -> 128 us
  Pallas kernels: 167 us -> 104 us
    pallas_call x4, Pallas kernels: 159 us -> 90.1 us  [the longest x1 35.2 us: gather(): pl.pallas_call(gather_kernel, out_shape=(jax.ShapeDtypeStruct((slots, 16,...]
    pallas_call x1, Pallas kernels: 8.84 us -> 14 us  [update(): pl.pallas_call(update_kernel, grid_spec=pltpu.PrefetchScalarGridSpec(num_...]
where the time goes in v2:
time: 129 us; the launch traced here: 128 us
  Pallas kernels  104 us (81%)
  between operations  16.7 us (13%)
  other arithmetic  2.63 us (2%)
  local copies, waits for them, and re-layouts  2.57 us (2%)
  matrix products  2.32 us (2%)
    pallas_call x1, Pallas kernels, gather(): pl.pallas_call(gather_kernel, out_shape=(jax.ShapeDtypeStruct((slots, 16,...  35.2 us
    pallas_call x1, Pallas kernels, factor(): pl.pallas_call(factor_kernel, out_shape=jax.ShapeDtypeStruct((slots, 16,...  29.2 us
    pallas_call x1, Pallas kernels, share(): pl.pallas_call(share_kernel, out_shape=(jax.ShapeDtypeStruct((4, 2, slots...  22.4 us
    pallas_call x1, Pallas kernels, update(): pl.pallas_call(update_kernel, grid_spec=pltpu.PrefetchScalarGridSpec(num_...  14 us
    pallas_call x1, Pallas kernels, pick(): pl.pallas_call(pick_kernel, out_shape=jax.ShapeDtypeStruct((8, slots, 16,...  3.24 us

profile of v2, /device:TPU:3, one launch (start us, length us, event | category | flops | bytes accessed | tf_op | source)
XLA Modules:
  0.0 128.3 jit_solution(1699975941293658186)
XLA Ops:
  7.2 0.7 fusion.98
  7.8 1.0 fusion.105
  9.0 0.6 reduce_max.18
  9.6 0.8 fusion.101
  11.8 0.2 fusion.106
  12.0 0.1 copy.162
  12.1 0.1 reshape.259
  12.2 0.2 fusion.81
  12.7 0.1 reshape.255
  12.8 0.1 broadcast_maximum_fusion
  12.9 0.1 select_reduce_fusion.8
  14.1 0.2 fusion.88
  14.5 0.1 convert_element_type.127
  14.6 0.6 fusion.100
  15.2 0.2 convert_reduce_fusion
  16.1 0.8 constant_dynamic-slice_fusion.7
  16.9 0.3 dynamic-slice_reduce_fusion
  17.3 0.1 concatenate.27
  17.4 104.1 %conditional.1 = ((bf16[2,8,128,512]{3,2,1,0:T(8,128)(2,1)}, f32[8,16,128,128]{3,2,1,0:T(8,128)})) conditional(s32[]{:T(128)} %clamp.3, (s32[32]{0:T(128)S(1)}, f32[8,1,16,1,128,128]{5,4,3,2,1,0:T(8,128)}, s32[552]{0:T(1024)S(1)}, f32[8,16,128,128]{3,2,1,0:T(8,128)}) %tuple.147, (f32[8,1,16,1,128,128]{5,4,3,2,1,0:T(8,128)}, ...), branch_computations={%region_11.12_spmd, %region_12.13_spmd, %region_13.36_spmd} | conditional | flops 9155118080 | bytes 461954624 | solution.py:744
  17.4 3.2 %pick.2 = f32[8,16,16,128]{3,2,1,0:T(8,128)S(1)} custom-call(s32[552]{0:T(1024)S(1)} %get-tuple-element.30.meta, f32[8,16,8,16,128]{4,3,2,1,0:T(8,128)} %bitcast.279), custom_call_target="tpu_custom_call" | custom-call | tf_op jit(solution)/shard_map/cond/branch_0_fun/pick/pallas_call | solution.py:68
  20.7 35.2 %gather.5 = (f32[16,16,128]{2,1,0:T(8,128)S(1)}, f32[4,2,256,128]{3,2,1,0:T(8,128)S(1)}) custom-call(s32[16]{0:T(128)S(1)} %bitcast.313, f32[4,2,16,16,128]{4,3,2,1,0:T(8,128)S(1)} %bitcast.269), custom_call_target="tpu_custom_call" | custom-call | tf_op jit(solution)/shard_map/cond/branch_0_fun/gather/pallas_call | solution.py:204
  55.9 29.2 %factor.2.l_ref = bf16[16,16,128]{2,1,0:T(8,128)(2,1)S(1)} custom-call(s32[552]{0:T(1024)S(1)} %get-tuple-element.30.meta, f32[16,16,128]{2,1,0:T(8,128)S(1)} %get-tuple-element.34.x_ref, f32[8,16,16,128]{3,2,1,0:T(8,128)S(1)} %bitcast.273), custom_call_target="tpu_custom_call" | custom-call | tf_op jit(solution)/shard_map/cond/branch_0_fun/factor/pallas_call | solution.py:391
  85.1 22.4 %share.2 = (bf16[4,2,16,16,128]{4,3,2,1,0:T(8,128)(2,1)S(1)}, bf16[2,4,4,1,8,16,128]{6,5,4,3,2,1,0:T(8,128)(2,1)S(1)}) custom-call(bf16[16,16,128]{2,1,0:T(8,128)(2,1)S(1)} %factor.2.l_ref), custom_call_target="tpu_custom_call" | custom-call | tf_op jit(solution)/shard_map/cond/branch_0_fun/share/pallas_call | solution.py:533
  107.5 14.0 %update.2 = (bf16[2,8,128,512]{3,2,1,0:T(8,128)(2,1)}, f32[8,16,128,128]{3,2,1,0:T(8,128)}) custom-call(s32[552]{0:T(1024)S(1)} %get-tuple-element.30.meta, f32[8,16,128,128]{3,2,1,0:T(8,128)S(1)} %copy-done, bf16[8,16,16,128]{3,2,1,0:T(8,128)(2,1)S(1)} %bitcast.275, bf16[2,16,128,128]{3,2,1,0:T(8,128)(2,1)S(1)} %bitcast.272), custom_call_target="tpu_custom_call" | custom-call | tf_op jit(solution)/shard_map/cond/branch_0_fun/update/pallas_call | solution.py:592
  (25 shorter events, 1.2 us)
Async XLA Ops:
  17.4 90.1 %copy-start = (f32[8,16,128,128]{3,2,1,0:T(8,128)S(1)}, f32[8,16,128,128]{3,2,1,0:T(8,128)}, u32[]{:S(2)}) copy-start(f32[8,16,128,128]{3,2,1,0:T(8,128)} %get-tuple-element.31.a_ref) | copy-start | bytes 25165828 | tf_op jit(solution)/shard_map/cond

commit v3 on v2

--- a/solution.py
+++ b/solution.py
@@ -4,31 +4,28 @@
 import jax.numpy as jnp
 from jax import lax
 from jax.experimental import pallas as pl
-from jax.experimental.layout import Layout, with_layout_constraint
 from jax.experimental.pallas import tpu as pltpu
 from jax.sharding import PartitionSpec as P
 
 SUPER = 4
 GROUP = 4
 PICKS = 8
-TIERS = (16, 32)
+TIERS = (16, 32, 64)
 MESH = pl.DeviceIdType.MESH
 HIGH = lax.Precision.HIGHEST
 F32 = jnp.float32
 BF16 = jnp.bfloat16
 NT = (((1,), (1,)), ((), ()))
 
-POS = 0
-POSC = 64
-ALIVE = 192
-SAME = 256
-POSD = 320
-TARGET = 384
-LEVEL = 392
-PLACE = 400
-COUNT = 408
-DEPTH = 416
-HIT = 424
+LABEL = 8
+ELIM = 9
+TARGET = 10
+LEVEL = 11
+SPOT = 12
+COUNT = 13
+SOURCE = 14
+SIZES = 15
+SLOTD = 16
 
 
 def dot_nt(a, b):
@@ -36,13 +33,15 @@
 
 
 def pick_kernel(meta, a_ref, out_ref, sems):
+    my_row = lax.axis_index("row")
     my_col = lax.axis_index("col")
     out_ref[...] = jnp.zeros_like(out_ref)
 
     def copy(p):
-        slot = jnp.maximum(meta[POS + p], 0)
-        target = meta[TARGET + p % PICKS]
-        mine = (meta[POS + p] >= 0) & (target % 8 == my_col)
+        slot = meta[p % PICKS, p // PICKS * 16 + my_row]
+        target = meta[TARGET, p % PICKS]
+        mine = (slot >= 0) & (target % 8 == my_col)
+        slot = jnp.maximum(slot, 0)
         return mine, pltpu.make_async_copy(
             a_ref.at[p // PICKS, target // 8], out_ref.at[:, slot], sems.at[slot]
         )
@@ -71,7 +70,7 @@
         in_specs=[pl.BlockSpec(memory_space=pltpu.SMEM), pl.BlockSpec(memory_space=pl.ANY)],
         out_specs=pl.BlockSpec(memory_space=pltpu.VMEM),
         scratch_shapes=[pltpu.SemaphoreType.DMA((slots,))],
-        compiler_params=pltpu.CompilerParams(vmem_limit_bytes=16 << 20),
+        compiler_params=pltpu.CompilerParams(vmem_limit_bytes=24 << 20),
         name="pick",
     )(meta, blocks)
 
@@ -83,7 +82,7 @@
 
 
 def gather_kernel(
-    dl_ref, give_ref, x_ref, d_ref, ra, acc, rb, dsrc, rr, piece,
+    meta, give_ref, x_ref, d_ref, ra, acc, rb, dsrc, rr, piece,
     sa, qa, sb, qb, sc, qc, sd, qd, se, qe, sf, qf,
 ):
     slots = x_ref.shape[0]
@@ -132,7 +131,7 @@
     x_ref[...] = total
 
     for d in range(slots):
-        code = dl_ref[d]
+        code = meta[SOURCE, d]
         mine = (code // 64 == r).astype(F32)
         dsrc[d * 16 : (d + 1) * 16] = x_ref[code % 64] * mine
     parts = []
@@ -197,7 +196,7 @@
         h.wait_send()
 
 
-def gather(dl, given):
+def gather(meta, given):
     slots = given.shape[1]
     vmem = pl.BlockSpec(memory_space=pltpu.VMEM)
     dma = pltpu.SemaphoreType.DMA
@@ -221,10 +220,10 @@
             dma((4,)), dma((4,)), dma((4,)), dma((4,)),
         ],
         compiler_params=pltpu.CompilerParams(
-            collective_id=slots, has_side_effects=True, vmem_limit_bytes=32 << 20
+            collective_id=slots, has_side_effects=True, vmem_limit_bytes=48 << 20
         ),
         name="gather",
-    )(dl, given.reshape(4, 2, slots, 16, 128))
+    )(meta, given.reshape(4, 2, slots, 16, 128))
 
 
 def lane(x, i):
@@ -302,29 +301,29 @@
                     ht[rows] -= change[:, 128:]
 
 
-def factor_kernel(meta, x_ref, d_ref, out_ref, st, ht, ub, vb, g, f, s, w, ld):
+def factor_kernel(meta, x_ref, d_ref, out_ref, st, ht, ub, vb, g, f, s, w, ld, lf):
     def same(i, j):
-        return meta[SAME + i * PICKS + j] > 0
+        return meta[SLOTD + i, j] >= 0
 
     def held(value, i, j):
         return jnp.where(i // SUPER < j // SUPER, value.astype(BF16).astype(F32), value)
 
     def block(i, j):
-        return d_ref[:, meta[POSD + i * PICKS + j]].reshape(128, 128)
+        return d_ref[:, meta[SLOTD + i, j]].reshape(128, 128)
 
     st[...] = jnp.zeros_like(st)
     unit = lax.broadcasted_iota(jnp.int32, (128, 128), 0) == lax.broadcasted_iota(
         jnp.int32, (128, 128), 1
     )
 
-    @pl.loop(0, meta[DEPTH])
+    @pl.loop(0, meta[SIZES, 1])
     def _(level):
         for b in range(8):
             ht[b * 128 : (b + 1) * 128] = unit.astype(F32)
 
         @pl.loop(0, PICKS)
         def _(j):
-            @pl.when(meta[LEVEL + j] == level)
+            @pl.when(meta[LEVEL, j] == level)
             def _():
                 s[...] = block(j, j)
 
@@ -347,42 +346,55 @@
                         done = held(done, i, j)
                         s[...] -= dot_nt(done, done)
 
-                st[pl.ds(pl.multiple_of(meta[PLACE + j] * 128, 128), 128)] = s[...]
-
-        batched_inverse(st, ht, ub, vb, meta[COUNT + level])
+                st[pl.ds(pl.multiple_of(meta[SPOT, j] * 128, 128), 128)] = s[...]
+
+        batched_inverse(st, ht, ub, vb, meta[COUNT, level])
 
         @pl.loop(0, PICKS)
         def _(j):
-            @pl.when(meta[LEVEL + j] == level)
+            @pl.when(meta[LEVEL, j] == level)
             def _():
-                g[j] = ht[pl.ds(pl.multiple_of(meta[PLACE + j] * 128, 128), 128)]
-
+                g[j] = ht[pl.ds(pl.multiple_of(meta[SPOT, j] * 128, 128), 128)]
+
+    my_row = lax.axis_index("row")
     ld[...] = jnp.zeros_like(ld)
     out_ref[...] = jnp.zeros_like(out_ref)
 
     @pl.loop(0, 64)
     def _(p):
-        @pl.when(meta[POS + p] >= 0)
+        slot = meta[p % PICKS, p // PICKS * 16 + my_row]
+
+        @pl.when(slot >= 0)
         def _():
             a = pl.multiple_of(p // PICKS * 16, 16)
-            ld[p % PICKS, pl.ds(a, 16)] = x_ref[meta[POS + p]]
-
-    @pl.loop(0, PICKS)
+            ld[p % PICKS, pl.ds(a, 16)] = x_ref[slot]
+
+    for j in range(PICKS):
+        lf[j] = dot_nt(ld[j], g[j])
+
+    @pl.loop(1, PICKS)
     def _(j):
-        @pl.loop(0, j)
-        def _(i):
-            @pl.when(same(j, i))
-            def _():
-                ld[j] -= dot_nt(held(ld[i], i, j), held(f[j * PICKS + i], i, j))
-
-        ld[j] = dot_nt(ld[j], g[j])
+        @pl.when(meta[LEVEL, j] > 0)
+        def _():
+            @pl.loop(0, j)
+            def _(i):
+                @pl.when(same(j, i))
+                def _():
+                    ld[j] -= dot_nt(held(lf[i], i, j), held(f[j * PICKS + i], i, j))
+
+            lf[j] = dot_nt(ld[j], g[j])
 
     @pl.loop(0, 64)
     def _(p):
-        @pl.when((meta[POS + p] >= 0) & (meta[ALIVE + p] > 0))
+        here = p // PICKS * 16 + my_row
+        slot = meta[p % PICKS, here]
+        elim = meta[ELIM, here]
+        alive = (elim < 0) | (elim >= (p % PICKS // SUPER + 1) * SUPER)
+
+        @pl.when((slot >= 0) & alive)
         def _():
             a = pl.multiple_of(p // PICKS * 16, 16)
-            out_ref[meta[POS + p]] = ld[p % PICKS, pl.ds(a, 16)].astype(BF16)
+            out_ref[slot] = lf[p % PICKS, pl.ds(a, 16)].astype(BF16)
 
 
 def factor(meta, x, d):
@@ -403,8 +415,9 @@
             pltpu.VMEM((128, 128), F32),
             pltpu.VMEM((128, 128), F32),
             pltpu.VMEM((8, 128, 128), F32),
+            pltpu.VMEM((8, 128, 128), F32),
         ],
-        compiler_params=pltpu.CompilerParams(vmem_limit_bytes=32 << 20),
+        compiler_params=pltpu.CompilerParams(vmem_limit_bytes=48 << 20),
         name="factor",
     )(meta, x, d.reshape(8, slots, 16, 128))
 
@@ -543,7 +556,7 @@
             dma((7,)), dma((7,)), dma((7,)), dma((7,)),
         ],
         compiler_params=pltpu.CompilerParams(
-            collective_id=slots + 1, has_side_effects=True, vmem_limit_bytes=32 << 20
+            collective_id=slots + 1, has_side_effects=True, vmem_limit_bytes=48 << 20
         ),
         name="share",
     )(l)
@@ -551,8 +564,10 @@
 
 def update_kernel(meta, a_ref, row_ref, col_ref, panel_ref, out_ref):
     a = pl.program_id(0)
+    my_col = lax.axis_index("col")
+    g = a * 16 + lax.axis_index("row")
     for j in range(PICKS):
-        slot = meta[POS + a * PICKS + j]
+        slot = meta[j, g]
         lanes = slice((j % SUPER) * 128, (j % SUPER + 1) * 128)
 
         @pl.when(slot >= 0)
@@ -564,7 +579,8 @@
             panel_ref[j // SUPER, 0, :, lanes] = jnp.zeros((128, 128), BF16)
 
     for b in range(16):
-        hit = meta[HIT + a * 16 + b] > 0
+        h = b * 8 + my_col
+        hit = meta[LABEL, g] == meta[LABEL, h]
 
         @pl.when(hit)
         def _():
@@ -572,13 +588,12 @@
 
             @pl.loop(0, PICKS)
             def _(j):
-                slot = meta[POS + a * PICKS + j]
+                slot = meta[j, g]
 
                 @pl.when(slot >= 0)
                 def _():
                     left = row_ref[:, slot].reshape(128, 128)
-                    down = meta[POSC + (b % 2) * 64 + (b // 2) * PICKS + j]
-                    right = col_ref[b % 2, jnp.maximum(down, 0)]
+                    right = col_ref[b % 2, jnp.maximum(meta[j, h], 0)]
                     out_ref[0, b] -= lax.dot_general(left, right, NT, preferred_element_type=F32)
 
         @pl.when(jnp.logical_not(hit))
@@ -608,140 +623,97 @@
             jax.ShapeDtypeStruct((2, 8, 128, 512), BF16),
             jax.ShapeDtypeStruct((8, 16, 128, 128), F32),
         ),
-        compiler_params=pltpu.CompilerParams(vmem_limit_bytes=32 << 20),
+        compiler_params=pltpu.CompilerParams(vmem_limit_bytes=48 << 20),
         name="update",
     )(meta, blocks, rows.reshape(8, slots, 16, 128), cols.reshape(2, slots, 128, 128))
 
 
-def tables(pattern, order, my_row, my_col):
-    target = order[:PICKS]
-    blocks = jnp.arange(128, dtype=jnp.int32)
-    onehot = (target[:, None] == blocks[None, :]).astype(F32)
-    linked = pattern.astype(F32)
-    member = jnp.dot(onehot, linked)
-    among = jnp.dot(member, onehot.T)
-    index = jnp.arange(64, dtype=jnp.int32)
-    before = (index[:, None] < index[None, :]).astype(F32)
-    own = member.reshape(PICKS, 8, 16).transpose(2, 1, 0).reshape(16, 64)
-    rank = jnp.dot(own, before)
-    slot = jnp.where(own > 0, rank, -1.0)
-    full = jnp.max(jnp.sum(own, axis=1))
-    small = jnp.arange(PICKS)
-    low = (small[None, :] <= small[:, None])
-    ed = (among.T * low).reshape(1, 64)
-    rankd = jnp.dot(ed, before)
-    fulld = jnp.sum(ed)
-    ed2 = ed.reshape(PICKS, PICKS)
-    level = jnp.sum(ed2, axis=1).astype(jnp.int32) - 1
-    peers = level[:, None] == level[None, :]
-    spot = jnp.sum(peers & (small[None, :] < small[:, None]), axis=1)
-    count = jnp.sum(level[None, :] == small[:, None], axis=1)
-    by_block = slot.reshape(16, 8, PICKS).transpose(1, 0, 2).reshape(128, PICKS)
-    where_d = jnp.dot(onehot, by_block)
-    code = (target % 16)[:, None] * 64 + where_d.astype(jnp.int32)
-    code = jnp.where(ed2 > 0, code, 0).reshape(64)
-    rankd = jnp.where(ed > 0, rankd, -1.0).astype(jnp.int32).reshape(64)
-    slots = jnp.arange(TIERS[-1], dtype=jnp.int32)
-    match = rankd[None, :] == slots[:, None]
-    dl = jnp.where(
-        slots < fulld.astype(jnp.int32),
-        jnp.sum(jnp.where(match, code[None, :], 0), axis=1),
-        16 * 64,
-    )
-    dead = jnp.stack([jnp.sum(onehot[:SUPER], axis=0), jnp.sum(onehot, axis=0)])
-    alive = 1.0 - lax.dynamic_index_in_dim(dead.reshape(2, 8, 16), my_row, 2, keepdims=False)
-    alive = jnp.repeat(alive.T, SUPER, axis=1).reshape(64).astype(jnp.int32)
-    slot = slot.astype(jnp.int32)
-    hit = lax.dynamic_index_in_dim(pattern.reshape(8, 16, 128), my_row, 1, keepdims=False)
-    hit = lax.dynamic_index_in_dim(hit.reshape(8, 16, 8), my_col, 2, keepdims=False)
-    pick_row = lambda i: lax.dynamic_index_in_dim(slot, i, 0, keepdims=False)
-    meta = jnp.concatenate(
-        [
-            pick_row(my_row), pick_row(my_col), pick_row(my_col + 8), alive,
-            ed.astype(jnp.int32).reshape(64), jnp.maximum(rankd, 0),
-            target, level, spot, count, jnp.full((8,), jnp.max(level) + 1), hit.reshape(128),
-        ]
-    ).astype(jnp.int32)
-    need = jnp.maximum(full, fulld)
-    tier = sum((need > slots).astype(jnp.int32) for slots in TIERS)
-    return meta, dl.astype(jnp.int32), tier
-
-
-def compact(slots, meta, dl, blocks):
+def ranks(marks, before):
+    total = jnp.sum(marks, axis=0, keepdims=True)
+    run = jnp.dot(jnp.broadcast_to(total, (8, 128)), before, preferred_element_type=F32)[:1]
+    rows = []
+    for j in range(8):
+        rows.append(jnp.where(marks[j : j + 1] > 0, run, -1.0))
+        run = run + marks[j : j + 1]
+    return jnp.concatenate(rows, axis=0), jnp.max(run, axis=1, keepdims=True)
+
+
+def tables_kernel(order, pattern_ref, meta_ref):
+    lanes = lax.broadcasted_iota(jnp.int32, (8, 128), 1)
+    rows = lax.broadcasted_iota(jnp.int32, (8, 128), 0)
+    lane = lanes[:1]
+    g = lax.broadcasted_iota(jnp.int32, (128, 128), 0)
+    h = lax.broadcasted_iota(jnp.int32, (128, 128), 1)
+    onehot = jnp.zeros((8, 128), F32)
+    target = jnp.zeros((1, 128), jnp.int32)
+    for j in range(PICKS):
+        onehot = jnp.where((rows == j) & (lanes == order[j]), 1.0, onehot)
+        target = jnp.where(lane == j, order[j], target)
+    linked = pattern_ref[...].astype(F32)
+    pad = lambda x: jnp.concatenate([x, jnp.zeros((120, 128), F32)], axis=0)
+    small = lambda a, b: lax.dot_general(a, b, NT, preferred_element_type=F32)
+    member = jnp.dot(onehot, linked, preferred_element_type=F32)
+    slot, full = ranks(member, (((g & 15) == (h & 15)) & (g < h)).astype(F32))
+    among = small(onehot, pad(member))
+    lower = jnp.where(lanes <= rows, among, 0.0)
+    upper = jnp.where(rows <= lanes, among, 0.0)
+    slotd, fulld = ranks(lower, (g < h).astype(F32))
+    home = jnp.sum(onehot * (lanes & 15).astype(F32), axis=1, keepdims=True)
+    code = home * 64.0 + small(onehot, pad(slot))
+    source = jnp.zeros((8, 128), F32)
+    for j in range(PICKS):
+        source = source + jnp.where(slotd[:, j : j + 1] == lanes.astype(F32), code[:, j : j + 1], 0.0)
+    source = jnp.sum(source, axis=0, keepdims=True)
+    source = jnp.where(lane.astype(F32) < fulld, source, 1024.0)
+    down = jnp.sum(lower, axis=1, keepdims=True) - 1.0
+    level = jnp.sum(upper, axis=0, keepdims=True) - 1.0
+    spot = jnp.sum(jnp.where((down == level) & (rows < lanes), 1.0, 0.0), axis=0, keepdims=True)
+    count = jnp.sum(jnp.where(down == lanes.astype(F32), 1.0, 0.0), axis=0, keepdims=True)
+    depth = jnp.max(down, axis=0, keepdims=True) + 1.0
+    sizes = jnp.where(lane == 0, jnp.maximum(full, fulld), depth)
+    elim = jnp.sum(onehot * (rows + 1).astype(F32), axis=0, keepdims=True) - 1.0
+    label = jnp.min(jnp.where(linked > 0, g.astype(F32), 999.0), axis=0, keepdims=True)
+
+    def put(row, value):
+        meta_ref[row : row + value.shape[0]] = value.astype(jnp.int32)
+
+    put(0, slot)
+    put(LABEL, label)
+    put(ELIM, elim)
+    put(TARGET, target)
+    put(LEVEL, level)
+    put(SPOT, spot)
+    put(COUNT, count)
+    put(SOURCE, source)
+    put(SIZES, sizes)
+    put(SLOTD, slotd)
+
+
+def tables(pattern, order):
+    vmem = pl.BlockSpec(memory_space=pltpu.VMEM)
+    return pl.pallas_call(
+        tables_kernel,
+        out_shape=jax.ShapeDtypeStruct((24, 128), jnp.int32),
+        in_specs=[pl.BlockSpec(memory_space=pltpu.SMEM), vmem],
+        out_specs=vmem,
+        name="tables",
+    )(order, pattern)
+
+
+def compact(slots, meta, blocks):
     given = pick(slots, meta, blocks.reshape(8, 16, 8, 16, 128))
-    x, d = gather(dl[:slots], given)
+    x, d = gather(meta, given)
     l = factor(meta, x, d)
     rows, cols = share(l)
     return update(meta, blocks, rows, cols)
 
 
-def broadcast(value, axis, source):
-    kept = jnp.where(lax.axis_index(axis) == source, value, 0).astype(value.dtype)
-    return lax.psum(kept, axis)
-
-
-def dense(pattern, order, local):
-    rows_axis = lax.axis_size("row")
-    cols_axis = lax.axis_size("col")
-    my_row = lax.axis_index("row")
-    my_col = lax.axis_index("col")
-    row_blocks, col_blocks, _, width = local.shape
-    local = with_layout_constraint(local, Layout((0, 1, 2, 3)))
-    ratio = rows_axis // cols_axis
-    total_blocks = row_blocks * rows_axis
-    my_pattern = lax.dynamic_index_in_dim(
-        pattern.reshape(row_blocks, rows_axis, total_blocks), my_row, 1, keepdims=False
-    )
-    my_pattern = lax.dynamic_index_in_dim(
-        my_pattern.reshape(row_blocks, col_blocks, cols_axis), my_col, 2, keepdims=False
-    )
-    current = local * my_pattern.astype(F32)[:, :, None, None]
-    dead = jnp.zeros((total_blocks,), F32)
-    results = []
-    for step in range(2):
-        chosen = order[step * SUPER : (step + 1) * SUPER]
-        pieces = []
-        for member in range(SUPER):
-            target = chosen[member]
-            column_here = lax.dynamic_index_in_dim(current, target // cols_axis, 1, keepdims=False)
-            pieces.append(broadcast(column_here, "col", target % cols_axis))
-        panel = jnp.concatenate(pieces, axis=2)
-        parts_list = []
-        for member in range(SUPER):
-            target = chosen[member]
-            row_here = lax.dynamic_index_in_dim(panel, target // rows_axis, 0, keepdims=False)
-            parts_list.append(
-                jnp.where(target % rows_axis == my_row, row_here, jnp.zeros_like(row_here))
-            )
-        square = lax.psum(jnp.concatenate(parts_list, axis=0), "row")
-        factored = jnp.linalg.cholesky(square)
-        flat = panel.reshape(row_blocks * width, SUPER * width)
-        lower = lax.linalg.triangular_solve(
-            factored, flat, left_side=False, lower=True, transpose_a=True
-        )
-        dead = dead.at[chosen].set(1.0)
-        alive = lax.dynamic_index_in_dim(
-            (1.0 - dead).reshape(row_blocks, rows_axis), my_row, 1, keepdims=False
-        )
-        rounded = (lower.reshape(row_blocks, width, SUPER * width) * alive[:, None, None]).astype(
-            BF16
-        )
-        results.append(rounded)
-        whole = lax.all_gather(rounded, "row", axis=0, tiled=True)
-        whole = whole.reshape(ratio, cols_axis, row_blocks, width, SUPER * width)
-        picked = lax.dynamic_index_in_dim(whole, my_col, 1, keepdims=False)
-        column_panel = picked.transpose(1, 0, 2, 3).reshape(col_blocks, width, SUPER * width)
-        change = jnp.einsum("aik,cjk->acij", rounded, column_panel, preferred_element_type=F32)
-        current = current - change
-    panels = with_layout_constraint(jnp.stack(results), Layout((0, 1, 2, 3)))
-    return panels, with_layout_constraint(current, Layout((0, 1, 2, 3)))
-
-
 def shards(matrix_blocks, pattern, order):
     local = matrix_blocks[:, 0, :, 0]
-    meta, dl, tier = tables(pattern, order, lax.axis_index("row"), lax.axis_index("col"))
-    ways = [functools.partial(compact, slots, meta, dl, local) for slots in TIERS]
-    panels, trailing = lax.switch(tier, ways + [lambda: dense(pattern, order, local)])
+    meta = tables(pattern, order)
+    tier = sum((meta[SIZES, 0] > slots).astype(jnp.int32) for slots in TIERS[:-1])
+    ways = [functools.partial(compact, slots, meta, local) for slots in TIERS]
+    panels, trailing = lax.switch(tier, ways)
     return panels[:, :, None], trailing[:, None, :, None]
 
 

time: 129 us -> 102 us (0.79)
  between operations: 16.7 us -> 1.94 us
  Pallas kernels: 104 us -> 98.4 us
  other arithmetic: 2.63 us -> 0 us
  matrix products: 2.32 us -> 0 us
  local copies, waits for them, and re-layouts: 2.57 us -> 0.52 us
    pallas_call x1, Pallas kernels: 29.2 us -> 23.5 us  [factor(): pl.pallas_call(factor_kernel, out_shape=jax.ShapeDtypeStruct((slots, 16,...]
    dot_general x5 -> x0, matrix products: 2.32 us -> none  [the longest x1 1.03 us: tables(): member = jnp.dot(onehot, linked)]
    pallas_call x1, Pallas kernels: 14 us -> 11.9 us  [update(): pl.pallas_call(update_kernel, grid_spec=pltpu.PrefetchScalarGridSpec(num_...]
    pallas_call x0 -> x1, Pallas kernels: none -> 1.36 us  [tables(): pl.pallas_call(tables_kernel, out_shape=jax.ShapeDtypeStruct((24, 128), j...]
where the time goes in v3:
time: 102 us; the launch traced here: 101 us
  Pallas kernels  98.4 us (96%)
  between operations  1.94 us (2%)
    pallas_call x1, Pallas kernels, gather(): pl.pallas_call(gather_kernel, out_shape=(jax.ShapeDtypeStruct((slots, 16,...  35.4 us
    pallas_call x1, Pallas kernels, factor(): pl.pallas_call(factor_kernel, out_shape=jax.ShapeDtypeStruct((slots, 16,...  23.5 us
    pallas_call x1, Pallas kernels, share(): pl.pallas_call(share_kernel, out_shape=(jax.ShapeDtypeStruct((4, 2, slots...  22.4 us
    pallas_call x1, Pallas kernels, update(): pl.pallas_call(update_kernel, grid_spec=pltpu.PrefetchScalarGridSpec(num_...  11.9 us
    pallas_call x1, Pallas kernels, pick(): pl.pallas_call(pick_kernel, out_shape=jax.ShapeDtypeStruct((8, slots, 16,...  3.8 us

profile of v3, /device:TPU:3, one launch (start us, length us, event | category | flops | bytes accessed | tf_op | source)
XLA Modules:
  0.0 100.9 jit_solution(18228534387989471212)
XLA Ops:
  0.6 1.4 %tables.1 = s32[24,128]{1,0:T(8,128)S(1)} custom-call(s32[128]{0:T(128)} %order.1, s32[128,128]{1,0:T(8,128)} %pattern_ref.1), custom_call_target="tpu_custom_call" | custom-call | tf_op jit(solution)/shard_map/tables/pallas_call | solution.py:694
  2.0 0.5 slice.5
  3.8 97.1 %conditional.1 = ((bf16[2,8,128,512]{3,2,1,0:T(8,128)(2,1)}, f32[8,16,128,128]{3,2,1,0:T(8,128)})) conditional(s32[]{:T(128)} %bitcast.21, (f32[8,1,16,1,128,128]{5,4,3,2,1,0:T(8,128)}, s32[24,128]{1,0:T(8,128)S(1)}, f32[8,16,128,128]{3,2,1,0:T(8,128)}) %tuple.39, (f32[8,1,16,1,128,128]{5,4,3,2,1,0:T(8,128)}, ...), branch_computations={%region_0.0_spmd, %region_1.0_spmd, %region_2.0_spmd} | conditional | bytes 41943124 | solution.py:716
  3.8 0.0 copy-start.1
  3.8 3.8 %pick.3 = f32[8,16,16,128]{3,2,1,0:T(8,128)S(1)} custom-call(s32[24,128]{1,0:T(8,128)S(1)} %get-tuple-element.26.meta, f32[8,16,8,16,128]{4,3,2,1,0:T(8,128)} %bitcast.39), custom_call_target="tpu_custom_call" | custom-call | tf_op jit(solution)/shard_map/cond/branch_0_fun/pick/pallas_call | solution.py:67
  7.6 35.4 %gather.3 = (f32[16,16,128]{2,1,0:T(8,128)S(1)}, f32[4,2,256,128]{3,2,1,0:T(8,128)S(1)}) custom-call(s32[24,128]{1,0:T(8,128)S(1)} %get-tuple-element.26.meta, f32[4,2,16,16,128]{4,3,2,1,0:T(8,128)S(1)} %bitcast.27), custom_call_target="tpu_custom_call" | custom-call | tf_op jit(solution)/shard_map/cond/branch_0_fun/gather/pallas_call | solution.py:203
  43.1 23.5 %factor.3.l_ref = bf16[16,16,128]{2,1,0:T(8,128)(2,1)S(1)} custom-call(s32[24,128]{1,0:T(8,128)S(1)} %get-tuple-element.26.meta, f32[16,16,128]{2,1,0:T(8,128)S(1)} %get-tuple-element.29.x_ref, f32[8,16,16,128]{3,2,1,0:T(8,128)S(1)} %bitcast.33), custom_call_target="tpu_custom_call" | custom-call | tf_op jit(solution)/shard_map/cond/branch_0_fun/factor/pallas_call | solution.py:403
  66.6 22.4 %share.3 = (bf16[4,2,16,16,128]{4,3,2,1,0:T(8,128)(2,1)S(1)}, bf16[2,4,4,1,8,16,128]{6,5,4,3,2,1,0:T(8,128)(2,1)S(1)}) custom-call(bf16[16,16,128]{2,1,0:T(8,128)(2,1)S(1)} %factor.3.l_ref), custom_call_target="tpu_custom_call" | custom-call | tf_op jit(solution)/shard_map/cond/branch_0_fun/share/pallas_call | solution.py:546
  89.0 0.0 copy-done.1
  89.0 11.9 %update.3 = (bf16[2,8,128,512]{3,2,1,0:T(8,128)(2,1)}, f32[8,16,128,128]{3,2,1,0:T(8,128)}) custom-call(s32[24,128]{1,0:T(8,128)S(1)} %get-tuple-element.26.meta, f32[8,16,128,128]{3,2,1,0:T(8,128)S(1)} %copy-done.1, bf16[8,16,16,128]{3,2,1,0:T(8,128)(2,1)S(1)} %bitcast.35, bf16[2,16,128,128]{3,2,1,0:T(8,128)(2,1)S(1)} %bitcast.34), custom_call_target="tpu_custom_call" | custom-call | tf_op jit(solution)/shard_map/cond/branch_0_fun/update/pallas_call | solution.py:607
Async XLA Ops:
  3.8 85.2 %copy-start.1 = (f32[8,16,128,128]{3,2,1,0:T(8,128)S(1)}, f32[8,16,128,128]{3,2,1,0:T(8,128)}, u32[]{:S(2)}) copy-start(f32[8,16,128,128]{3,2,1,0:T(8,128)} %get-tuple-element.27.a_ref) | copy-start | bytes 25165828 | tf_op jit(solution)/shard_map/cond

commit v4 on v3

--- a/solution.py
+++ b/solution.py
@@ -9,6 +9,7 @@
 
 SUPER = 4
 GROUP = 4
+AHEAD = 4
 PICKS = 8
 TIERS = (16, 32, 64)
 MESH = pl.DeviceIdType.MESH
@@ -25,6 +26,11 @@
 COUNT = 13
 SOURCE = 14
 SIZES = 15
+NUMBER = 24
+ONE = 25
+TWO = 26
+HITS = 27
+LIST = 32
 SLOTD = 16
 
 
@@ -37,30 +43,26 @@
     my_col = lax.axis_index("col")
     out_ref[...] = jnp.zeros_like(out_ref)
 
-    def copy(p):
-        slot = meta[p % PICKS, p // PICKS * 16 + my_row]
-        target = meta[TARGET, p % PICKS]
-        mine = (slot >= 0) & (target % 8 == my_col)
-        slot = jnp.maximum(slot, 0)
-        return mine, pltpu.make_async_copy(
-            a_ref.at[p // PICKS, target // 8], out_ref.at[:, slot], sems.at[slot]
-        )
-
-    @pl.loop(0, 64)
-    def _(p):
-        mine, c = copy(p)
-
-        @pl.when(mine)
-        def _():
-            c.start()
-
-    @pl.loop(0, 64)
-    def _(p):
-        mine, c = copy(p)
-
-        @pl.when(mine)
-        def _():
-            c.wait()
+    def each(act):
+        @pl.loop(0, PICKS)
+        def _(j):
+            target = meta[TARGET, j]
+
+            @pl.when(target % 8 == my_col)
+            def _():
+                for a in range(8):
+                    slot = meta[j, a * 16 + my_row]
+
+                    @pl.when(slot >= 0)
+                    def _():
+                        act(
+                            pltpu.make_async_copy(
+                                a_ref.at[a, target // 8], out_ref.at[:, slot], sems.at[slot]
+                            )
+                        )
+
+    each(lambda copy: copy.start())
+    each(lambda copy: copy.wait())
 
 
 def pick(slots, meta, blocks):
@@ -95,13 +97,33 @@
     def across(dr):
         return {"row": lax.rem(r + dr, 16), "col": c}
 
+    z, x = r // 4, lax.rem(r, 4)
+
+    def along_x(d):
+        return {"row": z * 4 + lax.rem(x + d, 4), "col": c}
+
+    def along_z(d):
+        return {"row": lax.rem(z + d, 4) * 4 + x, "col": c}
+
+    inside = y // 2 == k
+
+    def to_half(dy):
+        return {"row": r, "col": lax.rem(y + dy, 4) * 2 + y // 2}
+
     barrier = pltpu.get_barrier_semaphore()
     pl.semaphore_signal(barrier, inc=1, device_id=other, device_id_type=MESH)
     for dy in (1, 2, 3):
         pl.semaphore_signal(barrier, inc=1, device_id=along(dy), device_id_type=MESH)
     for dr in range(1, 16):
         pl.semaphore_signal(barrier, inc=1, device_id=across(dr), device_id_type=MESH)
-    pl.semaphore_wait(barrier, 19)
+    for q in range(4):
+        @pl.when(4 * k + q != c)
+        def _():
+            pl.semaphore_signal(
+                barrier, inc=1, device_id={"row": r, "col": 4 * k + q}, device_id_type=MESH
+            )
+
+    pl.semaphore_wait(barrier, 22 + jnp.where(inside, 0, 1))
 
     halves = []
     for dy in (2, 1, 3, 0):
@@ -147,53 +169,90 @@
     for dr, h in zip(range(1, 16), parts):
         h.wait_recv()
         total = total + rr[dr]
-    piece[...] = total
-    mine = pl.ds(pl.multiple_of(r * slots, 8), slots)
-    d_ref[y, k, mine] = total
-    wholes = []
-    for dr in range(1, 16):
+    piece[...] = total.reshape(piece.shape)
+
+    outs = []
+    for dy in (2, 1, 3):
         h = pltpu.make_async_remote_copy(
-            src_ref=piece, dst_ref=d_ref.at[y, k, mine],
-            send_sem=sd.at[dr], recv_sem=qd.at[dr], device_id=across(dr), device_id_type=MESH,
+            src_ref=piece, dst_ref=d_ref.at[z, x, :, c],
+            send_sem=sd.at[dy], recv_sem=qd.at[c], device_id=to_half(dy), device_id_type=MESH,
         )
         h.start()
-        wholes.append(h)
-    for h in wholes:
+        outs.append(h)
+    near = pltpu.make_async_remote_copy(
+        src_ref=piece, dst_ref=d_ref.at[z, x, :, c],
+        send_sem=sd.at[0], recv_sem=qd.at[c], device_id=other, device_id_type=MESH,
+    )
+
+    @pl.when(inside)
+    def _():
+        d_ref[z, x, :, c] = piece[...]
+
+    @pl.when(jnp.logical_not(inside))
+    def _():
+        near.start()
+
+    for q in range(4):
+        source = 4 * k + q
+
+        @pl.when(source != c)
+        def _():
+            pltpu.make_async_remote_copy(
+                src_ref=piece, dst_ref=d_ref.at[z, x, :, source],
+                send_sem=sd.at[0], recv_sem=qd.at[source], device_id=other, device_id_type=MESH,
+            ).wait_recv()
+
+    def move(ref, i, device):
+        h = pltpu.make_async_remote_copy(
+            src_ref=ref, dst_ref=ref, send_sem=se.at[i], recv_sem=qe.at[i],
+            device_id=device, device_id_type=MESH,
+        )
+        h.start()
+        return h
+
+    def twin(ref, i):
+        h = pltpu.make_async_remote_copy(
+            src_ref=ref, dst_ref=ref, send_sem=sf.at[i], recv_sem=qf.at[i],
+            device_id=other, device_id_type=MESH,
+        )
+        h.start()
+        twins.append(h)
+
+    part_x, part_z = pl.ds(4 * k, 2), pl.ds(4 * k + 2, 2)
+    near_x, near_z, far_x, far_z, twins = [], [], [], [], []
+    for d in (2, 1, 3):
+        near_x.append(move(d_ref.at[z, x, :, part_x], d, along_x(d)))
+        near_z.append(move(d_ref.at[z, x, :, part_z], 4 + d, along_z(d)))
+    for h in near_x:
         h.wait_recv()
-    spread(d_ref, along, other, y, k, se, qe, sf, qf)
+    for d in (2, 1, 3):
+        far_x.append((d, move(d_ref.at[z, :, :, part_x], 8 + d, along_z(d))))
+    for h in near_z:
+        h.wait_recv()
+    for d in (2, 1, 3):
+        far_z.append((d, move(d_ref.at[:, x, :, part_z], 12 + d, along_x(d))))
+    twin(d_ref.at[z, :, :, part_x], 0)
+    twin(d_ref.at[:, x, :, part_z], 4)
+    for i in (1, 2, 0):
+        d, h = far_x[i]
+        h.wait_recv()
+        twin(d_ref.at[lax.rem(z + 4 - d, 4), :, :, part_x], d)
+        d, h = far_z[i]
+        h.wait_recv()
+        twin(d_ref.at[:, lax.rem(x + 4 - d, 4), :, part_z], 4 + d)
+    wholes = near_x + near_z + [h for _, h in far_x + far_z]
+    for t in twins:
+        t.wait()
     for _, _, h in halves:
         h.wait_send()
     for _, q in quarters:
         q.wait_send()
-    for h in parts + wholes:
+    for h in parts + wholes + outs:
         h.wait_send()
 
-
-def spread(ref, along, other, y, k, se, qe, sf, qf):
-    outs = []
-    for dy in (2, 1, 3):
-        h = pltpu.make_async_remote_copy(
-            src_ref=ref.at[y, k], dst_ref=ref.at[y, k],
-            send_sem=se.at[dy], recv_sem=qe.at[dy], device_id=along(dy), device_id_type=MESH,
-        )
-        h.start()
-        outs.append((dy, h))
-    twins = []
-    for dy in (0, 1, 3, 2):
-        come = lax.rem(y + 4 - dy, 4)
-        for d, h in outs:
-            if d == dy:
-                h.wait_recv()
-        t = pltpu.make_async_remote_copy(
-            src_ref=ref.at[come, k], dst_ref=ref.at[come, k],
-            send_sem=sf.at[dy], recv_sem=qf.at[dy], device_id=other, device_id_type=MESH,
-        )
-        t.start()
-        twins.append(t)
-    for t in twins:
-        t.wait()
-    for _, h in outs:
-        h.wait_send()
+    @pl.when(jnp.logical_not(inside))
+    def _():
+        near.wait_send()
 
 
 def gather(meta, given):
@@ -204,7 +263,7 @@
         gather_kernel,
         out_shape=(
             jax.ShapeDtypeStruct((slots, 16, 128), F32),
-            jax.ShapeDtypeStruct((4, 2, slots * 16, 128), F32),
+            jax.ShapeDtypeStruct((4, 4, slots // 16, 8, 16, 128), F32),
         ),
         in_specs=[pl.BlockSpec(memory_space=pltpu.SMEM), vmem],
         out_specs=(vmem, vmem),
@@ -214,10 +273,10 @@
             pltpu.VMEM((4, slots, 16, 128), F32),
             pltpu.VMEM((slots * 16, 128), F32),
             pltpu.VMEM((16, slots, 128), F32),
-            pltpu.VMEM((slots, 128), F32),
+            pltpu.VMEM((slots // 16, 16, 128), F32),
             dma((4,)), dma((4,)), dma((4,)), dma((4,)),
-            dma((16,)), dma((16,)), dma((16,)), dma((16,)),
-            dma((4,)), dma((4,)), dma((4,)), dma((4,)),
+            dma((16,)), dma((16,)), dma((4,)), dma((8,)),
+            dma((16,)), dma((16,)), dma((8,)), dma((8,)),
         ],
         compiler_params=pltpu.CompilerParams(
             collective_id=slots, has_side_effects=True, vmem_limit_bytes=48 << 20
@@ -309,7 +368,7 @@
         return jnp.where(i // SUPER < j // SUPER, value.astype(BF16).astype(F32), value)
 
     def block(i, j):
-        return d_ref[:, meta[SLOTD + i, j]].reshape(128, 128)
+        return d_ref[meta[SLOTD + i, j]]
 
     st[...] = jnp.zeros_like(st)
     unit = lax.broadcasted_iota(jnp.int32, (128, 128), 0) == lax.broadcasted_iota(
@@ -357,17 +416,11 @@
                 g[j] = ht[pl.ds(pl.multiple_of(meta[SPOT, j] * 128, 128), 128)]
 
     my_row = lax.axis_index("row")
-    ld[...] = jnp.zeros_like(ld)
-    out_ref[...] = jnp.zeros_like(out_ref)
-
-    @pl.loop(0, 64)
-    def _(p):
-        slot = meta[p % PICKS, p // PICKS * 16 + my_row]
-
-        @pl.when(slot >= 0)
-        def _():
-            a = pl.multiple_of(p // PICKS * 16, 16)
-            ld[p % PICKS, pl.ds(a, 16)] = x_ref[slot]
+    last = out_ref.shape[0] - 1
+    for a in range(8):
+        for j in range(PICKS):
+            slot = meta[j, a * 16 + my_row]
+            ld[j, a * 16 : (a + 1) * 16] = jnp.where(slot >= 0, x_ref[jnp.maximum(slot, 0)], 0.0)
 
     for j in range(PICKS):
         lf[j] = dot_nt(ld[j], g[j])
@@ -384,17 +437,13 @@
 
             lf[j] = dot_nt(ld[j], g[j])
 
-    @pl.loop(0, 64)
-    def _(p):
-        here = p // PICKS * 16 + my_row
-        slot = meta[p % PICKS, here]
-        elim = meta[ELIM, here]
-        alive = (elim < 0) | (elim >= (p % PICKS // SUPER + 1) * SUPER)
-
-        @pl.when((slot >= 0) & alive)
-        def _():
-            a = pl.multiple_of(p // PICKS * 16, 16)
-            out_ref[slot] = lf[p % PICKS, pl.ds(a, 16)].astype(BF16)
+    for a in range(8):
+        elim = meta[ELIM, a * 16 + my_row]
+        for j in range(PICKS):
+            slot = meta[j, a * 16 + my_row]
+            alive = (elim < 0) | (elim >= (j // SUPER + 1) * SUPER)
+            rows = jnp.where(alive, lf[j, a * 16 : (a + 1) * 16], 0.0)
+            out_ref[jnp.where(slot >= 0, slot, last)] = rows.astype(BF16)
 
 
 def factor(meta, x, d):
@@ -402,7 +451,7 @@
     vmem = pl.BlockSpec(memory_space=pltpu.VMEM)
     return pl.pallas_call(
         factor_kernel,
-        out_shape=jax.ShapeDtypeStruct((slots, 16, 128), BF16),
+        out_shape=jax.ShapeDtypeStruct((slots + 1, 16, 128), BF16),
         in_specs=[pl.BlockSpec(memory_space=pltpu.SMEM), vmem, vmem],
         out_specs=vmem,
         scratch_shapes=[
@@ -419,11 +468,12 @@
         ],
         compiler_params=pltpu.CompilerParams(vmem_limit_bytes=48 << 20),
         name="factor",
-    )(meta, x, d.reshape(8, slots, 16, 128))
+    )(meta, x, d.reshape(slots, 128, 128))
 
 
 def share_kernel(l_ref, row_ref, col_ref, se, qe, sf, qf, sg, qg, sx, qx, sz, qz):
-    n = l_ref.shape[0] // 16
+    slots = l_ref.shape[0] - 1
+    n = slots // 16
     r, c, y, k = place()
     z, x = r // 4, lax.rem(r, 4)
     other = {"row": r, "col": y * 2 + 1 - k}
@@ -478,7 +528,7 @@
     def _():
         send(0).start()
 
-    row_ref[y, k] = l_ref[...]
+    row_ref[y, k] = l_ref[:slots]
     outs = []
     for d in (2, 1, 3):
         h = pltpu.make_async_remote_copy(
@@ -540,7 +590,7 @@
 
 
 def share(l):
-    slots = l.shape[0]
+    slots = l.shape[0] - 1
     vmem = pl.BlockSpec(memory_space=pltpu.VMEM)
     dma = pltpu.SemaphoreType.DMA
     return pl.pallas_call(
@@ -562,43 +612,79 @@
     )(l)
 
 
-def update_kernel(meta, a_ref, row_ref, col_ref, panel_ref, out_ref):
+def update_kernel(meta, a_ref, row_ref, col_ref, panel_ref, out_ref, held, sems):
     a = pl.program_id(0)
     my_col = lax.axis_index("col")
-    g = a * 16 + lax.axis_index("row")
-    for j in range(PICKS):
-        slot = meta[j, g]
-        lanes = slice((j % SUPER) * 128, (j % SUPER + 1) * 128)
-
-        @pl.when(slot >= 0)
+    my_row = lax.axis_index("row")
+
+    def fetch(a, n):
+        b = meta[LIST + n, a * 16 + my_row]
+        place = lax.rem(a, AHEAD)
+        return pltpu.make_async_copy(a_ref.at[a, b], held.at[place, n], sems.at[place, n])
+
+    def ask(a):
+        @pl.loop(0, meta[HITS, a * 16 + my_row])
+        def _(n):
+            fetch(a, n).start()
+
+    @pl.when(a == 0)
+    def _():
+        for t in range(AHEAD - 1):
+            ask(t)
+
+    @pl.when(a < 9 - AHEAD)
+    def _():
+        ask(a + AHEAD - 1)
+
+    g = a * 16 + my_row
+    panel_ref[...] = jnp.zeros_like(panel_ref)
+    out_ref[...] = jnp.zeros_like(out_ref)
+    number = meta[NUMBER, g]
+
+    def left(slot):
+        return row_ref[:, slot].reshape(128, 128)
+
+    def product(x, y):
+        return lax.dot_general(x, y, NT, preferred_element_type=F32)
+
+    @pl.when(number > 0)
+    def _():
+        for j in range(PICKS):
+            @pl.when(meta[j, g] >= 0)
+            def _():
+                lanes = slice((j % SUPER) * 128, (j % SUPER + 1) * 128)
+                panel_ref[j // SUPER, 0, :, lanes] = left(meta[j, g])
+
+    @pl.loop(0, meta[HITS, g])
+    def _(n):
+        b = meta[LIST + n, g]
+        h = b * 8 + my_col
+        half = lax.rem(b, 2)
+        fetch(a, n).wait()
+        value = held.at[lax.rem(a, AHEAD), n]
+
+        @pl.when(number == 0)
         def _():
-            panel_ref[j // SUPER, 0, :, lanes] = row_ref[:, slot].reshape(128, 128)
-
-        @pl.when(slot < 0)
+            out_ref[0, b] = value[...]
+
+        @pl.when(number == 1)
         def _():
-            panel_ref[j // SUPER, 0, :, lanes] = jnp.zeros((128, 128), BF16)
-
-    for b in range(16):
-        h = b * 8 + my_col
-        hit = meta[LABEL, g] == meta[LABEL, h]
-
-        @pl.when(hit)
+            out_ref[0, b] = value[...] - product(left(meta[ONE, g]), col_ref[half, meta[ONE, h]])
+
+        @pl.when(number >= 2)
         def _():
-            out_ref[0, b] = a_ref[0, b]
-
+            out_ref[0, b] = value[...] - product(
+                jnp.concatenate([left(meta[ONE, g]), left(meta[TWO, g])], axis=1),
+                jnp.concatenate([col_ref[half, meta[ONE, h]], col_ref[half, meta[TWO, h]]], axis=1),
+            )
+
+        @pl.when(number >= 3)
+        def _():
             @pl.loop(0, PICKS)
             def _(j):
-                slot = meta[j, g]
-
-                @pl.when(slot >= 0)
+                @pl.when((meta[j, g] >= 0) & (meta[LEVEL, j] >= 2))
                 def _():
-                    left = row_ref[:, slot].reshape(128, 128)
-                    right = col_ref[b % 2, jnp.maximum(meta[j, h], 0)]
-                    out_ref[0, b] -= lax.dot_general(left, right, NT, preferred_element_type=F32)
-
-        @pl.when(jnp.logical_not(hit))
-        def _():
-            out_ref[0, b] = jnp.zeros((128, 128), F32)
+                    out_ref[0, b] -= product(left(meta[j, g]), col_ref[half, meta[j, h]])
 
 
 def update(meta, blocks, rows, cols):
@@ -610,13 +696,17 @@
             num_scalar_prefetch=1,
             grid=(8,),
             in_specs=[
-                pl.BlockSpec((1, 16, 128, 128), lambda a, m: (a, 0, 0, 0)),
+                pl.BlockSpec(memory_space=pl.ANY),
                 pl.BlockSpec((8, slots, 16, 128), whole(4)),
                 pl.BlockSpec((2, slots, 128, 128), whole(4)),
             ],
             out_specs=[
                 pl.BlockSpec((2, 1, 128, 512), lambda a, m: (0, a, 0, 0)),
                 pl.BlockSpec((1, 16, 128, 128), lambda a, m: (a, 0, 0, 0)),
+            ],
+            scratch_shapes=[
+                pltpu.VMEM((AHEAD, 16, 128, 128), F32),
+                pltpu.SemaphoreType.DMA((AHEAD, 16)),
             ],
         ),
         out_shape=(
@@ -687,13 +777,29 @@
     put(SOURCE, source)
     put(SIZES, sizes)
     put(SLOTD, slotd)
+    rows16 = lax.broadcasted_iota(jnp.int32, (16, 128), 0)
+    lanes16 = lax.broadcasted_iota(jnp.int32, (16, 128), 1)
+    mine = (lanes16 == rows16 * 8 + lax.axis_index("col")).astype(F32)
+    held = jnp.dot(mine, linked, preferred_element_type=F32)
+    run = jnp.zeros((1, 128), F32)
+    listed = jnp.zeros((16, 128), F32)
+    for b in range(16):
+        here = held[b : b + 1]
+        listed = jnp.where((here > 0) & (run == rows16.astype(F32)), float(b), listed)
+        run = run + here
+    put(HITS, run)
+    put(LIST, listed)
+    put(NUMBER, jnp.sum(member, axis=0, keepdims=True))
+    for row, order_in in ((ONE, 0.0), (TWO, 1.0)):
+        taken = jnp.where((member > 0) & (down == order_in), slot + 1.0, 0.0)
+        put(row, jnp.sum(taken, axis=0, keepdims=True) - 1.0)
 
 
 def tables(pattern, order):
     vmem = pl.BlockSpec(memory_space=pltpu.VMEM)
     return pl.pallas_call(
         tables_kernel,
-        out_shape=jax.ShapeDtypeStruct((24, 128), jnp.int32),
+        out_shape=jax.ShapeDtypeStruct((48, 128), jnp.int32),
         in_specs=[pl.BlockSpec(memory_space=pltpu.SMEM), vmem],
         out_specs=vmem,
         name="tables",

time: 102 us -> 97.8 us (0.959)
  Pallas kernels: 98.4 us -> 94.7 us
    pallas_call x2, Pallas kernels: 24.9 us -> 19.2 us  [the longest x1 17.9 us: factor(): pl.pallas_call(factor_kernel, out_shape=jax.ShapeDtypeStruct((slots + 1,...]
    pallas_call x1, Pallas kernels: 11.9 us -> 14.1 us  [update(): pl.pallas_call(update_kernel, grid_spec=pltpu.PrefetchScalarGridSpec(num_...]
    pallas_call x1, Pallas kernels: 3.8 us -> 2.55 us  [pick(): pl.pallas_call(pick_kernel, out_shape=jax.ShapeDtypeStruct((8, slots, 16,...]
    pallas_call x1, Pallas kernels: 35.4 us -> 36.5 us  [gather(): pl.pallas_call(gather_kernel, out_shape=(jax.ShapeDtypeStruct((slots, 16,...]
where the time goes in v4:
time: 97.8 us; the launch traced here: 97.6 us
  Pallas kernels  94.7 us (97%)
  between operations  2.12 us (2%)
    pallas_call x1, Pallas kernels, gather(): pl.pallas_call(gather_kernel, out_shape=(jax.ShapeDtypeStruct((slots, 16,...  36.5 us
    pallas_call x1, Pallas kernels, share(): pl.pallas_call(share_kernel, out_shape=(jax.ShapeDtypeStruct((4, 2, slots...  22.3 us
    pallas_call x1, Pallas kernels, factor(): pl.pallas_call(factor_kernel, out_shape=jax.ShapeDtypeStruct((slots + 1,...  17.9 us
    pallas_call x1, Pallas kernels, update(): pl.pallas_call(update_kernel, grid_spec=pltpu.PrefetchScalarGridSpec(num_...  14.1 us
    pallas_call x1, Pallas kernels, pick(): pl.pallas_call(pick_kernel, out_shape=jax.ShapeDtypeStruct((8, slots, 16,...  2.55 us

profile of v4, /device:TPU:3, one launch (start us, length us, event | category | flops | bytes accessed | tf_op | source)
XLA Modules:
  0.0 97.6 jit_solution(12227777736384245859)
XLA Ops:
  0.6 1.3 %tables.1 = s32[48,128]{1,0:T(8,128)S(1)} custom-call(s32[128]{0:T(128)} %order.1, s32[128,128]{1,0:T(8,128)} %pattern_ref.1), custom_call_target="tpu_custom_call" | custom-call | tf_op jit(solution)/shard_map/tables/pallas_call | solution.py:800
  2.0 0.5 slice.5
  3.8 93.6 %conditional.1 = ((bf16[2,8,128,512]{3,2,1,0:T(8,128)(2,1)}, f32[8,16,128,128]{3,2,1,0:T(8,128)})) conditional(s32[]{:T(128)} %bitcast.21, (f32[8,1,16,1,128,128]{5,4,3,2,1,0:T(8,128)}, s32[48,128]{1,0:T(8,128)S(1)}, f32[8,16,128,128]{3,2,1,0:T(8,128)}) %tuple.39, (f32[8,1,16,1,128,128]{5,4,3,2,1,0:T(8,128)}, ...), branch_computations={%region_0.0_spmd, %region_1.0_spmd, %region_2.0_spmd} | conditional | bytes 41943124 | solution.py:822
  3.8 0.0 copy-start.1
  3.8 2.5 %pick.3 = f32[8,16,16,128]{3,2,1,0:T(8,128)S(1)} custom-call(s32[48,128]{1,0:T(8,128)S(1)} %get-tuple-element.26.meta, f32[8,16,8,16,128]{4,3,2,1,0:T(8,128)} %bitcast.39), custom_call_target="tpu_custom_call" | custom-call | tf_op jit(solution)/shard_map/cond/branch_0_fun/pick/pallas_call | solution.py:69
  6.4 36.5 %gather.3 = (f32[16,16,128]{2,1,0:T(8,128)S(1)}, f32[4,4,1,8,16,128]{5,4,3,2,1,0:T(8,128)S(1)}) custom-call(s32[48,128]{1,0:T(8,128)S(1)} %get-tuple-element.26.meta, f32[4,2,16,16,128]{4,3,2,1,0:T(8,128)S(1)} %bitcast.28), custom_call_target="tpu_custom_call" | custom-call | tf_op jit(solution)/shard_map/cond/branch_0_fun/gather/pallas_call | solution.py:262
  42.9 17.9 %factor.3.l_ref = bf16[17,16,128]{2,1,0:T(8,128)(2,1)S(1)} custom-call(s32[48,128]{1,0:T(8,128)S(1)} %get-tuple-element.26.meta, f32[16,16,128]{2,1,0:T(8,128)S(1)} %get-tuple-element.29.x_ref, f32[16,128,128]{2,1,0:T(8,128)S(1)} %bitcast.33), custom_call_target="tpu_custom_call" | custom-call | tf_op jit(solution)/shard_map/cond/branch_0_fun/factor/pallas_call | solution.py:452
  60.8 22.3 %share.3 = (bf16[4,2,16,16,128]{4,3,2,1,0:T(8,128)(2,1)S(1)}, bf16[2,4,4,1,8,16,128]{6,5,4,3,2,1,0:T(8,128)(2,1)S(1)}) custom-call(bf16[17,16,128]{2,1,0:T(8,128)(2,1)S(1)} %factor.3.l_ref), custom_call_target="tpu_custom_call" | custom-call | tf_op jit(solution)/shard_map/cond/branch_0_fun/share/pallas_call | solution.py:596
  83.1 0.0 copy-done.1
  83.1 14.1 %update.3 = (bf16[2,8,128,512]{3,2,1,0:T(8,128)(2,1)}, f32[8,16,128,128]{3,2,1,0:T(8,128)}) custom-call(s32[48,128]{1,0:T(8,128)S(1)} %get-tuple-element.26.meta, f32[8,16,128,128]{3,2,1,0:T(8,128)S(1)} %copy-done.1, bf16[8,16,16,128]{3,2,1,0:T(8,128)(2,1)S(1)} %bitcast.35, bf16[2,16,128,128]{3,2,1,0:T(8,128)(2,1)S(1)} %bitcast.34), custom_call_target="tpu_custom_call" | custom-call | tf_op jit(solution)/shard_map/cond/branch_0_fun/update/pallas_call | solution.py:693
Async XLA Ops:
  3.8 79.3 %copy-start.1 = (f32[8,16,128,128]{3,2,1,0:T(8,128)S(1)}, f32[8,16,128,128]{3,2,1,0:T(8,128)}, u32[]{:S(2)}) copy-start(f32[8,16,128,128]{3,2,1,0:T(8,128)} %get-tuple-element.27.a_ref) | copy-start | bytes 25165828 | tf_op jit(solution)/shard_map/cond

commit v5 on v4

--- a/solution.py
+++ b/solution.py
@@ -8,8 +8,7 @@
 from jax.sharding import PartitionSpec as P
 
 SUPER = 4
-GROUP = 4
-AHEAD = 4
+WAVE = 4
 PICKS = 8
 TIERS = (16, 32, 64)
 MESH = pl.DeviceIdType.MESH
@@ -23,7 +22,6 @@
 TARGET = 10
 LEVEL = 11
 SPOT = 12
-COUNT = 13
 SOURCE = 14
 SIZES = 15
 NUMBER = 24
@@ -286,6 +284,8 @@
 
 
 def lane(x, i):
+    if isinstance(i, int):
+        return jnp.broadcast_to(x[:, i : i + 1], x.shape)
     return jnp.take_along_axis(x, jnp.full(x.shape, i, jnp.int32), axis=1)
 
 
@@ -320,14 +320,14 @@
     return high, middle, (x - middle.astype(F32)).astype(BF16)
 
 
-def batched_inverse(st, ht, ub, vb, count):
-    lanes = lax.broadcasted_iota(jnp.int32, (16, 128), 1)
-
-    @pl.loop(0, 8)
-    def _(c):
-        base = c * 16
+def batched_inverse(st, ub, vb):
+    lanes = lax.broadcasted_iota(jnp.int32, (8, 128), 1)
+    for c in range(8):
+        base, end = c * 16, c * 16 + 16
         us = [st[pl.ds(base + k, 8, stride=128)] for k in range(16)]
-        vs = [ht[pl.ds(base + k, 8, stride=128)] for k in range(16)]
+        vs = [
+            jnp.where(lanes < base, us[k], (lanes == base + k).astype(F32)) for k in range(16)
+        ]
         us[:8], vs[:8] = pivots(us[:8], vs[:8], base)
         for m in range(8, 16):
             for k in range(8):
@@ -336,31 +336,37 @@
                 vs[m] = vs[m] - w * vs[k]
         us[8:], vs[8:] = pivots(us[8:], vs[8:], base + 8)
         for k in range(16):
-            ht[pl.ds(base + k, 8, stride=128)] = vs[k]
-            ub[pl.ds(k, 8, stride=16)] = us[k]
-            vb[pl.ds(k, 8, stride=16)] = vs[k]
-
-        @pl.when(c < 7)
-        def _():
-            @pl.loop(0, (count + GROUP - 1) // GROUP)
-            def _(q):
-                for t in range(GROUP):
-                    b = q * GROUP + t
-                    here = pl.ds(pl.multiple_of(b * 16, 16), 16)
-                    u = ub[here]
-                    x, y, z = split(jnp.where(lanes >= base + 16, u, 0.0))
-                    left = jnp.concatenate([x, x, y, y, x, z], axis=0)
-                    x, y, z = split(jnp.concatenate([u, vb[here]], axis=1))
-                    right = jnp.concatenate([x, y, x, y, z, x], axis=0)
-                    change = lax.dot_general(
-                        left, right, (((0,), (0,)), ((), ())), preferred_element_type=F32
-                    )
-                    rows = pl.ds(pl.multiple_of(b * 128, 128), 128)
-                    st[rows] -= change[:, :128]
-                    ht[rows] -= change[:, 128:]
-
-
-def factor_kernel(meta, x_ref, d_ref, out_ref, st, ht, ub, vb, g, f, s, w, ld, lf):
+            st[pl.ds(base + k, 8, stride=128)] = vs[k]
+            ub[pl.ds(k, 8, stride=16)] = jnp.where(lanes < end, 0.0, us[k])
+            vb[pl.ds(k, 8, stride=16)] = jnp.where(lanes < end, vs[k], us[k])
+        if c == 7:
+            continue
+        tall = lax.broadcasted_iota(jnp.int32, (128 - end, 128), 1)
+        passed = (tall >= base) & (tall < end)
+        for b in range(8):
+            here = slice(b * 16, b * 16 + 16)
+            x, y, z = split(ub[here])
+            left = jnp.concatenate([x, x, y, y, x, z], axis=0)
+            x, y, z = split(vb[here])
+            right = jnp.concatenate([x, y, x, y, z, x], axis=0)
+            change = lax.dot_general(
+                left, right, (((0,), (0,)), ((), ())), preferred_element_type=F32
+            )
+            rows = slice(b * 128 + end, b * 128 + 128)
+            st[rows] = jnp.where(passed, 0.0, st[rows]) - change[end:]
+
+
+def factor_kernel(
+    meta, x_ref, d_ref, out_ref, panel_ref, trailing_ref, st, ub, vb, g, f, s, w, ld, lf,
+    blank, empty, sems,
+):
+    blank[...] = jnp.zeros_like(blank)
+    empty[...] = jnp.zeros_like(empty)
+    fills = [pltpu.make_async_copy(blank, trailing_ref.at[a], sems.at[a]) for a in range(8)]
+    fills += [pltpu.make_async_copy(empty, panel_ref.at[p], sems.at[8 + p]) for p in range(2)]
+    for fill in fills:
+        fill.start()
+
     def same(i, j):
         return meta[SLOTD + i, j] >= 0
 
@@ -371,15 +377,8 @@
         return d_ref[meta[SLOTD + i, j]]
 
     st[...] = jnp.zeros_like(st)
-    unit = lax.broadcasted_iota(jnp.int32, (128, 128), 0) == lax.broadcasted_iota(
-        jnp.int32, (128, 128), 1
-    )
-
     @pl.loop(0, meta[SIZES, 1])
     def _(level):
-        for b in range(8):
-            ht[b * 128 : (b + 1) * 128] = unit.astype(F32)
-
         @pl.loop(0, PICKS)
         def _(j):
             @pl.when(meta[LEVEL, j] == level)
@@ -407,13 +406,13 @@
 
                 st[pl.ds(pl.multiple_of(meta[SPOT, j] * 128, 128), 128)] = s[...]
 
-        batched_inverse(st, ht, ub, vb, meta[COUNT, level])
+        batched_inverse(st, ub, vb)
 
         @pl.loop(0, PICKS)
         def _(j):
             @pl.when(meta[LEVEL, j] == level)
             def _():
-                g[j] = ht[pl.ds(pl.multiple_of(meta[SPOT, j] * 128, 128), 128)]
+                g[j] = st[pl.ds(pl.multiple_of(meta[SPOT, j] * 128, 128), 128)]
 
     my_row = lax.axis_index("row")
     last = out_ref.shape[0] - 1
@@ -445,17 +444,23 @@
             rows = jnp.where(alive, lf[j, a * 16 : (a + 1) * 16], 0.0)
             out_ref[jnp.where(slot >= 0, slot, last)] = rows.astype(BF16)
 
+    for fill in fills:
+        fill.wait()
+
 
 def factor(meta, x, d):
     slots = x.shape[0]
     vmem = pl.BlockSpec(memory_space=pltpu.VMEM)
     return pl.pallas_call(
         factor_kernel,
-        out_shape=jax.ShapeDtypeStruct((slots + 1, 16, 128), BF16),
+        out_shape=(
+            jax.ShapeDtypeStruct((slots + 1, 16, 128), BF16),
+            jax.ShapeDtypeStruct((2, 8, 8, 16, 512), BF16),
+            jax.ShapeDtypeStruct((8, 16, 128, 128), F32),
+        ),
         in_specs=[pl.BlockSpec(memory_space=pltpu.SMEM), vmem, vmem],
-        out_specs=vmem,
+        out_specs=(vmem, pl.BlockSpec(memory_space=pl.ANY), pl.BlockSpec(memory_space=pl.ANY)),
         scratch_shapes=[
-            pltpu.VMEM((1024, 128), F32),
             pltpu.VMEM((1024, 128), F32),
             pltpu.VMEM((128, 128), F32),
             pltpu.VMEM((128, 128), F32),
@@ -465,6 +470,9 @@
             pltpu.VMEM((128, 128), F32),
             pltpu.VMEM((8, 128, 128), F32),
             pltpu.VMEM((8, 128, 128), F32),
+            pltpu.VMEM((16, 128, 128), F32),
+            pltpu.VMEM((8, 8, 16, 512), BF16),
+            pltpu.SemaphoreType.DMA((10,)),
         ],
         compiler_params=pltpu.CompilerParams(vmem_limit_bytes=48 << 20),
         name="factor",
@@ -612,34 +620,61 @@
     )(l)
 
 
-def update_kernel(meta, a_ref, row_ref, col_ref, panel_ref, out_ref, held, sems):
-    a = pl.program_id(0)
+def update_kernel(
+    meta, a_ref, row_in, col_in, zero_panel, zero, panel_ref, out_ref, held, done, row_ref, col_ref,
+    listed, come, go, out, bring,
+):
     my_col = lax.axis_index("col")
     my_row = lax.axis_index("row")
-
-    def fetch(a, n):
-        b = meta[LIST + n, a * 16 + my_row]
-        place = lax.rem(a, AHEAD)
-        return pltpu.make_async_copy(a_ref.at[a, b], held.at[place, n], sems.at[place, n])
-
-    def ask(a):
-        @pl.loop(0, meta[HITS, a * 16 + my_row])
-        def _(n):
-            fetch(a, n).start()
-
-    @pl.when(a == 0)
-    def _():
-        for t in range(AHEAD - 1):
-            ask(t)
-
-    @pl.when(a < 9 - AHEAD)
-    def _():
-        ask(a + AHEAD - 1)
-
-    g = a * 16 + my_row
-    panel_ref[...] = jnp.zeros_like(panel_ref)
-    out_ref[...] = jnp.zeros_like(out_ref)
-    number = meta[NUMBER, g]
+    rows_in = pltpu.make_async_copy(row_in, row_ref, bring.at[0])
+    cols_in = pltpu.make_async_copy(col_in, col_ref, bring.at[1])
+    rows_in.start()
+    cols_in.start()
+
+    def fetch(q):
+        code = listed[q]
+        return pltpu.make_async_copy(a_ref.at[code // 16, code % 16], held.at[q], come.at[q])
+
+    def store(q):
+        code = listed[q]
+        return pltpu.make_async_copy(done.at[q], out_ref.at[code // 16, code % 16], go.at[q])
+
+    def row(a, start):
+        g = a * 16 + my_row
+
+        def one(n, q):
+            listed[q] = a * 16 + meta[LIST + n, g]
+            fetch(q).start()
+            return q + 1
+
+        return lax.fori_loop(0, meta[HITS, g], one, start)
+
+    total = lax.fori_loop(0, 8, row, 0)
+
+    def each_panel(act):
+        @pl.loop(0, 8)
+        def _(a):
+            g = a * 16 + my_row
+
+            @pl.when(meta[NUMBER, g] > 0)
+            def _():
+                for j in range(PICKS):
+                    slot = meta[j, g]
+
+                    @pl.when(slot >= 0)
+                    def _():
+                        lanes = pl.ds((j % SUPER) * 128, 128)
+                        act(
+                            pltpu.make_async_copy(
+                                row_ref.at[:, slot],
+                                panel_ref.at[j // SUPER, a, :, :, lanes],
+                                out.at[slot],
+                            )
+                        )
+
+    rows_in.wait()
+    each_panel(lambda copy: copy.start())
+    cols_in.wait()
 
     def left(slot):
         return row_ref[:, slot].reshape(128, 128)
@@ -647,75 +682,86 @@
     def product(x, y):
         return lax.dot_general(x, y, NT, preferred_element_type=F32)
 
-    @pl.when(number > 0)
-    def _():
-        for j in range(PICKS):
-            @pl.when(meta[j, g] >= 0)
+    @pl.loop(0, (total + WAVE - 1) // WAVE)
+    def _(t):
+        for u in range(WAVE):
+            @pl.when(t * WAVE + u < total)
             def _():
-                lanes = slice((j % SUPER) * 128, (j % SUPER + 1) * 128)
-                panel_ref[j // SUPER, 0, :, lanes] = left(meta[j, g])
-
-    @pl.loop(0, meta[HITS, g])
-    def _(n):
-        b = meta[LIST + n, g]
-        h = b * 8 + my_col
-        half = lax.rem(b, 2)
-        fetch(a, n).wait()
-        value = held.at[lax.rem(a, AHEAD), n]
-
-        @pl.when(number == 0)
+                fetch(t * WAVE + u).wait()
+
+        places = [jnp.minimum(t * WAVE + u, total - 1) for u in range(WAVE)]
+        results = []
+        for q in places:
+            g = listed[q] // 16 * 16 + my_row
+            b = listed[q] % 16
+            h = b * 8 + my_col
+            half = b % 2
+            number = meta[NUMBER, g]
+            x, y = [], []
+            for t_row, least in ((ONE, 1), (TWO, 2)):
+                x.append(jnp.where(number >= least, left(jnp.maximum(meta[t_row, g], 0)), 0))
+                y.append(jnp.where(number >= least, col_ref[half, jnp.maximum(meta[t_row, h], 0)], 0))
+            results.append(
+                held[q] - product(jnp.concatenate(x, axis=1), jnp.concatenate(y, axis=1))
+            )
+        for q, result in zip(places, results):
+            done[q] = result
+
+        @pl.when(meta[SIZES, 1] > 2)
         def _():
-            out_ref[0, b] = value[...]
-
-        @pl.when(number == 1)
-        def _():
-            out_ref[0, b] = value[...] - product(left(meta[ONE, g]), col_ref[half, meta[ONE, h]])
-
-        @pl.when(number >= 2)
-        def _():
-            out_ref[0, b] = value[...] - product(
-                jnp.concatenate([left(meta[ONE, g]), left(meta[TWO, g])], axis=1),
-                jnp.concatenate([col_ref[half, meta[ONE, h]], col_ref[half, meta[TWO, h]]], axis=1),
-            )
-
-        @pl.when(number >= 3)
-        def _():
-            @pl.loop(0, PICKS)
-            def _(j):
-                @pl.when((meta[j, g] >= 0) & (meta[LEVEL, j] >= 2))
+            @pl.loop(t * WAVE, jnp.minimum(t * WAVE + WAVE, total))
+            def _(q):
+                g = listed[q] // 16 * 16 + my_row
+                b = listed[q] % 16
+
+                @pl.when(meta[NUMBER, g] > 2)
                 def _():
-                    out_ref[0, b] -= product(left(meta[j, g]), col_ref[half, meta[j, h]])
-
-
-def update(meta, blocks, rows, cols):
+                    @pl.loop(2, PICKS)
+                    def _(j):
+                        @pl.when((meta[j, g] >= 0) & (meta[LEVEL, j] >= 2))
+                        def _():
+                            done[q] -= product(
+                                left(meta[j, g]), col_ref[b % 2, meta[j, b * 8 + my_col]]
+                            )
+
+        for u in range(WAVE):
+            @pl.when(t * WAVE + u < total)
+            def _():
+                store(t * WAVE + u).start()
+
+    @pl.loop(0, total)
+    def _(q):
+        store(q).wait()
+
+    each_panel(lambda copy: copy.wait())
+
+
+def update(meta, blocks, rows, cols, panels, trailing):
     slots = rows.shape[2]
-    whole = lambda n: (lambda a, m: (0,) * n)
+    hbm = pl.BlockSpec(memory_space=pl.ANY)
     return pl.pallas_call(
         update_kernel,
-        grid_spec=pltpu.PrefetchScalarGridSpec(
-            num_scalar_prefetch=1,
-            grid=(8,),
-            in_specs=[
-                pl.BlockSpec(memory_space=pl.ANY),
-                pl.BlockSpec((8, slots, 16, 128), whole(4)),
-                pl.BlockSpec((2, slots, 128, 128), whole(4)),
-            ],
-            out_specs=[
-                pl.BlockSpec((2, 1, 128, 512), lambda a, m: (0, a, 0, 0)),
-                pl.BlockSpec((1, 16, 128, 128), lambda a, m: (a, 0, 0, 0)),
-            ],
-            scratch_shapes=[
-                pltpu.VMEM((AHEAD, 16, 128, 128), F32),
-                pltpu.SemaphoreType.DMA((AHEAD, 16)),
-            ],
+        out_shape=(
+            jax.ShapeDtypeStruct(panels.shape, BF16),
+            jax.ShapeDtypeStruct(trailing.shape, F32),
         ),
-        out_shape=(
-            jax.ShapeDtypeStruct((2, 8, 128, 512), BF16),
-            jax.ShapeDtypeStruct((8, 16, 128, 128), F32),
-        ),
+        in_specs=[pl.BlockSpec(memory_space=pltpu.SMEM), hbm, hbm, hbm, hbm, hbm],
+        out_specs=(hbm, hbm),
+        scratch_shapes=[
+            pltpu.VMEM((128, 128, 128), F32),
+            pltpu.VMEM((128, 128, 128), F32),
+            pltpu.VMEM((8, slots, 16, 128), BF16),
+            pltpu.VMEM((2, slots, 128, 128), BF16),
+            pltpu.SMEM((128,), jnp.int32),
+            pltpu.SemaphoreType.DMA((128,)),
+            pltpu.SemaphoreType.DMA((128,)),
+            pltpu.SemaphoreType.DMA((slots,)),
+            pltpu.SemaphoreType.DMA((2,)),
+        ],
+        input_output_aliases={4: 0, 5: 1},
         compiler_params=pltpu.CompilerParams(vmem_limit_bytes=48 << 20),
         name="update",
-    )(meta, blocks, rows.reshape(8, slots, 16, 128), cols.reshape(2, slots, 128, 128))
+    )(meta, blocks, rows.reshape(8, slots, 16, 128), cols.reshape(2, slots, 128, 128), panels, trailing)
 
 
 def ranks(marks, before):
@@ -728,7 +774,7 @@
     return jnp.concatenate(rows, axis=0), jnp.max(run, axis=1, keepdims=True)
 
 
-def tables_kernel(order, pattern_ref, meta_ref):
+def tables_kernel(order, pattern_ref, meta_ref, tier_ref):
     lanes = lax.broadcasted_iota(jnp.int32, (8, 128), 1)
     rows = lax.broadcasted_iota(jnp.int32, (8, 128), 0)
     lane = lanes[:1]
@@ -758,9 +804,11 @@
     down = jnp.sum(lower, axis=1, keepdims=True) - 1.0
     level = jnp.sum(upper, axis=0, keepdims=True) - 1.0
     spot = jnp.sum(jnp.where((down == level) & (rows < lanes), 1.0, 0.0), axis=0, keepdims=True)
-    count = jnp.sum(jnp.where(down == lanes.astype(F32), 1.0, 0.0), axis=0, keepdims=True)
     depth = jnp.max(down, axis=0, keepdims=True) + 1.0
-    sizes = jnp.where(lane == 0, jnp.maximum(full, fulld), depth)
+    need = jnp.maximum(full, fulld)
+    sizes = jnp.where(lane == 0, need, depth)
+    tier = sum((need > slots).astype(F32) for slots in TIERS[:-1])
+    tier_ref[0] = jnp.max(tier).astype(jnp.int32)
     elim = jnp.sum(onehot * (rows + 1).astype(F32), axis=0, keepdims=True) - 1.0
     label = jnp.min(jnp.where(linked > 0, g.astype(F32), 999.0), axis=0, keepdims=True)
 
@@ -773,7 +821,6 @@
     put(TARGET, target)
     put(LEVEL, level)
     put(SPOT, spot)
-    put(COUNT, count)
     put(SOURCE, source)
     put(SIZES, sizes)
     put(SLOTD, slotd)
@@ -799,9 +846,12 @@
     vmem = pl.BlockSpec(memory_space=pltpu.VMEM)
     return pl.pallas_call(
         tables_kernel,
-        out_shape=jax.ShapeDtypeStruct((48, 128), jnp.int32),
+        out_shape=(
+            jax.ShapeDtypeStruct((48, 128), jnp.int32),
+            jax.ShapeDtypeStruct((1,), jnp.int32),
+        ),
         in_specs=[pl.BlockSpec(memory_space=pltpu.SMEM), vmem],
-        out_specs=vmem,
+        out_specs=(vmem, pl.BlockSpec(memory_space=pltpu.SMEM)),
         name="tables",
     )(order, pattern)
 
@@ -809,17 +859,17 @@
 def compact(slots, meta, blocks):
     given = pick(slots, meta, blocks.reshape(8, 16, 8, 16, 128))
     x, d = gather(meta, given)
-    l = factor(meta, x, d)
+    l, panels, trailing = factor(meta, x, d)
     rows, cols = share(l)
-    return update(meta, blocks, rows, cols)
+    panels, trailing = update(meta, blocks, rows, cols, panels, trailing)
+    return panels.reshape(2, 8, 128, 512), trailing
 
 
 def shards(matrix_blocks, pattern, order):
     local = matrix_blocks[:, 0, :, 0]
-    meta = tables(pattern, order)
-    tier = sum((meta[SIZES, 0] > slots).astype(jnp.int32) for slots in TIERS[:-1])
+    meta, tier = tables(pattern, order)
     ways = [functools.partial(compact, slots, meta, local) for slots in TIERS]
-    panels, trailing = lax.switch(tier, ways)
+    panels, trailing = lax.switch(tier[0], ways)
     return panels[:, :, None], trailing[:, None, :, None]
 
 

time: 97.8 us -> 92.1 us (0.942)
  Pallas kernels: 94.7 us -> 89.3 us
    pallas_call x3, Pallas kernels: 33.3 us -> 28.3 us  [the longest x1 17 us: factor(): pl.pallas_call(factor_kernel, out_shape=(jax.ShapeDtypeStruct((slots + 1,...]
where the time goes in v5:
time: 92.1 us; the launch traced here: 91 us
  Pallas kernels  89.3 us (97%)
  between operations  1.47 us (2%)
    pallas_call x1, Pallas kernels, gather(): pl.pallas_call(gather_kernel, out_shape=(jax.ShapeDtypeStruct((slots, 16,...  36.3 us
    pallas_call x1, Pallas kernels, share(): pl.pallas_call(share_kernel, out_shape=(jax.ShapeDtypeStruct((4, 2, slots...  22.7 us
    pallas_call x1, Pallas kernels, factor(): pl.pallas_call(factor_kernel, out_shape=(jax.ShapeDtypeStruct((slots + 1,...  17 us
    pallas_call x1, Pallas kernels, update(): pl.pallas_call(update_kernel, out_shape=(jax.ShapeDtypeStruct(panels.shap...  9.4 us
    pallas_call x1, Pallas kernels, pick(): pl.pallas_call(pick_kernel, out_shape=jax.ShapeDtypeStruct((8, slots, 16,...  1.95 us
    pallas_call x1, Pallas kernels, tables(): pl.pallas_call(tables_kernel, out_shape=(jax.ShapeDtypeStruct((48, 128),...  1.88 us

profile of v5, /device:TPU:3, one launch (start us, length us, event | category | flops | bytes accessed | tf_op | source)
XLA Modules:
  0.0 91.0 jit_solution(4259189192526785986)
XLA Ops:
  0.6 1.9 %tables.1 = (s32[48,128]{1,0:T(8,128)S(1)}, s32[1]{0:T(128)}) custom-call(s32[128]{0:T(128)} %order.1, s32[128,128]{1,0:T(8,128)} %pattern_ref.1), custom_call_target="tpu_custom_call" | custom-call | tf_op jit(solution)/shard_map/tables/pallas_call | solution.py:847
  3.2 87.7 %conditional.1 = (f32[8,16,128,128]{3,2,1,0:T(8,128)}, bf16[2,8,1,128,512]{4,3,2,1,0:T(8,128)(2,1)}) conditional(s32[]{:T(128)} %bitcast.30, (f32[8,1,16,1,128,128]{5,4,3,2,1,0:T(8,128)}, s32[48,128]{1,0:T(8,128)S(1)}, f32[8,16,128,128]{3,2,1,0:T(8,128)}) %tuple.35, (f32[8,1,16,1,128,128]{5,4,3,2,1,0:T(8,128)}, ...), branch_computations={%region_0.0_spmd, %region_1.0_spmd, %region_2.0_spmd} | conditional | bytes 41943132 | solution.py:872
  3.2 0.0 copy-start.1
  3.2 2.0 %pick.3 = f32[8,16,16,128]{3,2,1,0:T(8,128)S(1)} custom-call(s32[48,128]{1,0:T(8,128)S(1)} %get-tuple-element.19.meta, f32[8,16,8,16,128]{4,3,2,1,0:T(8,128)} %bitcast.47), custom_call_target="tpu_custom_call" | custom-call | tf_op jit(solution)/shard_map/cond/branch_0_fun/pick/pallas_call | solution.py:67
  5.2 36.3 %gather.3 = (f32[16,16,128]{2,1,0:T(8,128)S(1)}, f32[4,4,1,8,16,128]{5,4,3,2,1,0:T(8,128)S(1)}) custom-call(s32[48,128]{1,0:T(8,128)S(1)} %get-tuple-element.19.meta, f32[4,2,16,16,128]{4,3,2,1,0:T(8,128)S(1)} %bitcast.36), custom_call_target="tpu_custom_call" | custom-call | tf_op jit(solution)/shard_map/cond/branch_0_fun/gather/pallas_call | solution.py:260
  41.5 17.0 %factor.3 = (bf16[17,16,128]{2,1,0:T(8,128)(2,1)S(1)}, bf16[2,8,8,16,512]{4,3,2,1,0:T(8,128)(2,1)}, f32[8,16,128,128]{3,2,1,0:T(8,128)}) custom-call(s32[48,128]{1,0:T(8,128)S(1)} %get-tuple-element.19.meta, f32[16,16,128]{2,1,0:T(8,128)S(1)} %get-tuple-element.22.x_ref, f32[16,128,128]{2,1,0:T(8,128)S(1)} %bitcast.41), custom_call_target="tpu_custom_call" | custom-call | tf_op jit(solution)/shard_map/cond/branch_0_fun/factor/pallas_call | solution.py:454
  58.5 22.7 %share.3 = (bf16[4,2,16,16,128]{4,3,2,1,0:T(8,128)(2,1)S(1)}, bf16[2,4,4,1,8,16,128]{6,5,4,3,2,1,0:T(8,128)(2,1)S(1)}) custom-call(bf16[17,16,128]{2,1,0:T(8,128)(2,1)S(1)} %get-tuple-element.24.l_ref), custom_call_target="tpu_custom_call" | custom-call | tf_op jit(solution)/shard_map/cond/branch_0_fun/share/pallas_call | solution.py:604
  81.2 0.0 copy-done.1
  81.2 9.4 %update.3 = (bf16[2,8,8,16,512]{4,3,2,1,0:T(8,128)(2,1)}, f32[8,16,128,128]{3,2,1,0:T(8,128)}) custom-call(s32[48,128]{1,0:T(8,128)S(1)} %get-tuple-element.19.meta, f32[8,16,128,128]{3,2,1,0:T(8,128)S(1)} %copy-done.1, bf16[8,16,16,128]{3,2,1,0:T(8,128)(2,1)S(1)} %bitcast.43, ...), custom_call_target="tpu_custom_call", output_to_operand_aliasing={{0}: (4, {}), {1}: (5, {})} | custom-call | tf_op jit(solution)/shard_map/cond/branch_0_fun/update/pallas_call | solution.py:742
Async XLA Ops:
  3.2 78.0 %copy-start.1 = (f32[8,16,128,128]{3,2,1,0:T(8,128)S(1)}, f32[8,16,128,128]{3,2,1,0:T(8,128)}, u32[]{:S(2)}) copy-start(f32[8,16,128,128]{3,2,1,0:T(8,128)} %get-tuple-element.20.a_ref) | copy-start | bytes 25165828 | tf_op jit(solution)/shard_map/cond
